TPU v7x, 32 devices: a whole 2x2x4 slice. The times are simulated.
32 devices in a mesh: tm: 8 (over z, y), eval: 4 (over x, core).
Axes of the slice: x: 2, y: 2, z: 4, core: 2. Of those that a mesh axis runs over, the one named last changes fastest.
Arguments:
- hidden: bfloat16 [128, 1024, 1536], P('tm', 'eval'), may hold values from -9 to 9
- modulation: float32 [128, 2, 1536], P('tm'), may hold values from -2 to 3
- head_weight: bfloat16 [64, 1536], replicated, may hold values from -1 to 1
- real_score: bfloat16 [32, 21, 16, 4096], P('eval', None, None, 'tm'), may hold values from -152917 to 152917
- fake_score: bfloat16 [32, 21, 16, 4096], P('eval', None, None, 'tm'), may hold values from -152917 to 152917
- window_start: int32 [32], P('eval'), may hold values from 0 to 107, as said below
- timestep: int32 [32], P('eval'), may hold values from 20 to 999
Outputs:
- d_hidden: bfloat16 [128, 1024, 1536], P('tm', 'eval')
- head_grad: float32 [64, 1536], replicated
- mod_grad: float32 [128, 2, 1536], P('tm')
Inputs may be any that keep to these rules, and one draw needn't show every extreme that they name: `window_start`: every window lies inside the rollout; one window starts at frame 0 and one at the last possible frame.
All inputs are finite; a program needn't handle non-finite values.
Results may differ from a plain program's by a relative error of at most 0.0012.
The roundings to bfloat16 on the way count: a program that leaves them out, or rounds other values in their place, can miss the bound.
Values may be sent and summed in bfloat16 or wider, within the bound.
A program may use at most 128 MiB of HBM per device.

v0:
```python
import jax
import jax.numpy as jnp
from jax import lax
from jax.sharding import PartitionSpec as P

C = 16
PATCH = 4
WIN = 21
TOK = 1024


def layer_norm(values_in):
    values = values_in.astype(jnp.float32)
    center = jnp.mean(values, axis=-1, keepdims=True)
    shifted = values - center
    inv_std = lax.rsqrt(jnp.mean(shifted * shifted, axis=-1, keepdims=True) + 1e-06)
    return (shifted * inv_std, inv_std)


def per_device(hidden, modulation, head_weight, real_score, fake_score, window_start, timestep):
    frames_dev, tok_dev, width = hidden.shape
    shift = modulation[:, 0][:, None, :]
    scale = modulation[:, 1][:, None, :]
    normed, inv_std = layer_norm(hidden)
    adapted = (normed * (1.0 + scale) + shift).astype(jnp.bfloat16)
    head_out = jnp.einsum("ftd,od->fto", adapted, head_weight, preferred_element_type=jnp.float32)
    latent = head_out.astype(jnp.bfloat16).reshape(frames_dev, tok_dev, C, PATCH)
    latent = latent.transpose(0, 2, 1, 3).reshape(frames_dev, C, tok_dev * PATCH)
    frame_whole = lax.all_gather(latent, "eval", axis=2, tiled=True)
    latent_all = lax.all_to_all(frame_whole, "tm", split_axis=2, concat_axis=0, tiled=True)
    pixel_block = latent_all.shape[2]
    frame_index = window_start[:, None] + jnp.arange(WIN, dtype=jnp.int32)[None, :]
    window_latent = latent_all[frame_index].astype(jnp.float32)
    real_values = real_score.astype(jnp.float32)
    fake_values = fake_score.astype(jnp.float32)
    abs_sums = jnp.sum(jnp.abs(window_latent - real_values), axis=(1, 2, 3))
    totals = lax.psum(abs_sums, "tm")
    normalizer = totals / (WIN * C * PATCH * TOK) + 1e-05
    weight = timestep.astype(jnp.float32) / 1000.0 / normalizer
    window_grad = weight[:, None, None, None] * (fake_values - real_values)
    group_grad = (
        jnp.zeros(latent_all.shape, jnp.float32)
        .at[frame_index.reshape(-1)]
        .add(window_grad.reshape(-1, C, pixel_block))
    )
    reduced = lax.psum_scatter(group_grad, "eval", scatter_dimension=2, tiled=True)
    home = lax.all_to_all(reduced, "tm", split_axis=0, concat_axis=2, tiled=True)
    n_time = lax.axis_size("tm")
    sub_block = reduced.shape[2]
    blocked = home.reshape(frames_dev, C, n_time, 1, sub_block)
    regrouped = lax.all_to_all(blocked, "eval", split_axis=2, concat_axis=3, tiled=True)
    owner_grad = regrouped.reshape(frames_dev, C, tok_dev * PATCH)
    upstream = owner_grad.reshape(frames_dev, C, tok_dev, PATCH).transpose(0, 2, 1, 3)
    upstream = upstream.reshape(frames_dev, tok_dev, C * PATCH).astype(jnp.bfloat16)
    d_adapted = jnp.einsum("fto,od->ftd", upstream, head_weight, preferred_element_type=jnp.float32)
    head_part = jnp.einsum("fto,ftd->od", upstream, adapted, preferred_element_type=jnp.float32)
    mod_part = jnp.stack([jnp.sum(d_adapted, axis=1), jnp.sum(d_adapted * normed, axis=1)], axis=1)
    head_grad = lax.psum(head_part, ("tm", "eval"))
    mod_grad = lax.psum(mod_part, "eval")
    d_normed = d_adapted * (1.0 + scale)
    d_hidden = inv_std * (
        d_normed
        - jnp.mean(d_normed, axis=-1, keepdims=True)
        - normed * jnp.mean(d_normed * normed, axis=-1, keepdims=True)
    )
    return (d_hidden.astype(jnp.bfloat16), head_grad, mod_grad)


def solution(mesh):
    placed = (
        P("tm", "eval", None),
        P("tm", None, None),
        P(),
        P("eval", None, None, "tm"),
        P("eval", None, None, "tm"),
        P("eval"),
        P("eval"),
    )
    return jax.shard_map(
        per_device,
        mesh=mesh,
        in_specs=placed,
        out_specs=(P("tm", "eval", None), P(), P("tm", None, None)),
        check_vma=False,
    )
```

profile of v0, /device:TPU:1, one launch (start us, length us, event | category | flops | bytes accessed | tf_op | source)
XLA Modules:
  0.0 543.9 jit_solution(2420196849811462487)
XLA Ops:
  7.2 6.4 %convert_reduce_fusion = f32[16,256]{1,0:T(8,128)S(1)} fusion(bf16[16,256,1536]{2,1,0:T(8,128)(2,1)} %param.7), kind=kLoop, calls=%fused_computation.3 | loop fusion | flops 12578816 | bytes 12599296 | tf_op jit(solution)/shard_map/reduce_sum | solution.py:14
  13.6 8.0 %fusion.13 = f32[16,256]{1,0:T(8,128)S(1)} fusion(bf16[16,256,1536]{2,1,0:T(8,128)(2,1)} %param.7, f32[16,256]{1,0:T(8,128)S(1)} %broadcast_multiply_fusion.2), kind=kLoop, calls=%fused_computation.17 | loop fusion | flops 25161728 | bytes 12615680 | tf_op jit(solution)/shard_map/reduce_sum | solution.py:16
  21.9 8.4 %fusion.24 = bf16[16,256,64]{1,2,0:T(8,128)(2,1)S(1)} fusion(bf16[16,256,1536]{2,1,0:T(8,128)(2,1)} %param.7, f32[16,1536]{1,0:T(8,128)S(1)} %get-tuple-element.28, f32[16,1536]{1,0:T(8,128)S(1)} %get-tuple-element.29, f32[16,256]{1,0:T(8,128)S(1)} %add_rsqrt_fusion, f32[16,256]{1,0:T(8,128)S(1)} %broadcast_multiply_fusion.2, bf16[64,1536]{1,0:T(8,128)(2,1)S(1)} %copy-done), kind=kOutput, calls=%fused_computation.27 | convolution fusion | flops 843317248 | bytes 13533184 | tf_op jit(solution)/shard_map/ftd,od->fto/dot_general | solution.py:26
  30.4 6.5 %copy.52 = bf16[16,256,16,4]{2,0,3,1:T(8,128)(2,1)} copy(bf16[16,256,16,4]{1,3,2,0:T(4,128)(2,1)S(1)} %reshape.113) | data formatting | bytes 1048576 | tf_op jit(solution)/shard_map/reshape | solution.py:27
  36.9 5.1 copy.53
  42.1 25.2 %all-gather.2.cloned.1.call-done = bf16[16,16,4096]{2,1,0:T(8,128)(2,1)} async-done(((bf16[16,16,1024]{2,1,0:T(8,128)(2,1)}), bf16[16,16,4096]{2,1,0:T(8,128)(2,1)}) %all-gather.2.cloned.1.call-update) | async-done | bytes 2097168 | tf_op jit(solution)/shard_map/all_gather | solution.py:29
  67.3 15.4 %copy.54 = bf16[16,16,4096]{1,0,2:T(8,128)(2,1)} copy(bf16[16,16,4096]{2,1,0:T(8,128)(2,1)} %all-gather.2.cloned.1.call-done) | data formatting | bytes 4194304 | tf_op jit(solution)/shard_map/all_gather | solution.py:29
  82.7 19.6 %reshape.137 = bf16[8,2,65536]{2,1,0:T(2,128)(2,1)} reshape(bf16[4096,16,16]{2,1,0:T(8,128)(2,1)} %bitcast.50) | data formatting | bytes 4194304
  102.2 5.2 all-to-all-start
  107.8 47.5 %all-to-all-done = bf16[8,2,65536]{2,1,0:T(2,128)(2,1)S(1)} async-done(((bf16[8,2,65536]{2,1,0:T(2,128)(2,1)}), bf16[8,2,65536]{2,1,0:T(2,128)(2,1)S(1)}, u32[]{:S(2)}, u32[]{:S(2)}) %all-to-all-start) | async-done | bytes 2097184 | tf_op jit(solution)/shard_map/all_to_all | solution.py:30
  155.3 13.1 %reshape.138 = bf16[4096,16,16]{2,1,0:T(8,128)(2,1)} reshape(bf16[8,2,65536]{2,1,0:T(2,128)(2,1)S(1)} %all-to-all-done) | data formatting | bytes 4194304
  168.4 16.0 %copy.56 = bf16[8,16,16,512]{3,2,1,0:T(8,128)(2,1)S(1)} copy(bf16[8,16,16,512]{2,1,3,0:T(8,128)(2,1)} %bitcast.51) | data formatting | bytes 4194304 | tf_op jit(solution)/shard_map/all_to_all | solution.py:30
  184.4 2.5 gather_fusion
  186.9 3.7 fusion.19
  190.6 16.6 %psum.21 = f32[8]{0:T(128)S(1)} all-reduce(f32[8]{0:T(128)S(1)} %fusion.19), channel_id=1, replica_groups=mesh['tm'=8,'eval'=4] {'tm'}, use_global_device_ids=true, to_apply=%region_3.0 | all-reduce | flops 8 | bytes 64 | tf_op jit(solution)/shard_map/psum | solution.py:37
  207.2 6.4 %fusion.20 = f32[8,21,16,512]{3,2,1,0:T(8,128)} fusion(bf16[8,21,16,512]{3,2,1,0:T(8,128)(2,1)} %param.10, bf16[8,21,16,512]{3,2,1,0:T(8,128)(2,1)} %param.11, f32[8]{0:T(128)S(1)} %add_divide_fusion), kind=kLoop, calls=%fused_computation.25 | loop fusion | flops 5505024 | bytes 11010080 | tf_op jit(solution)/shard_map/mul | solution.py:40
  213.6 2.5 broadcast_in_dim.2
  216.1 27.3 %scatter_fusion = f32[128,16,512]{2,1,0:T(8,128)} fusion(f32[128,16,512]{2,1,0:T(8,128)} %broadcast_in_dim.2, s32[168]{0:T(256)S(1)} %bitcast.61, f32[168,16,512]{2,1,0:T(8,128)} %bitcast.52), kind=kCustom, calls=%fused_computation.1 | custom fusion | flops 1376256 | bytes 16515744 | tf_op jit(solution)/shard_map/scatter-add | solution.py:44
  243.5 44.5 %reduce-scatter.2.cloned.1.call-done = f32[128,16,128]{2,1,0:T(8,128)} async-done(((f32[128,16,512]{2,1,0:T(8,128)}), f32[128,16,128]{2,1,0:T(8,128)}) %reduce-scatter.2.cloned.1.call-update) | async-done | bytes 1048592 | tf_op jit(solution)/shard_map/reduce_scatter | solution.py:46
  288.0 30.2 %all_to_all.46 = f32[128,16,128]{2,1,0:T(8,128)S(1)} all-to-all(f32[128,16,128]{2,1,0:T(8,128)} %reduce-scatter.2.cloned.1.call-done), channel_id=1, replica_groups=mesh['tm'=8,'eval'=4] {'tm'}, dimensions={0} | all-to-all | bytes 2097152 | tf_op jit(solution)/shard_map/all_to_all | solution.py:47
  318.1 17.6 %all_to_all.47 = f32[16,16,8,1,128]{4,1,0,3,2:T(8,128)S(1)} all-to-all(f32[16,16,8,1,128]{4,1,0,3,2:T(8,128)S(1)} %bitcast.57), channel_id=1, replica_groups=mesh['tm'=8,'eval'=4] {'eval'}, dimensions={2} | all-to-all | bytes 2097152 | tf_op jit(solution)/shard_map/all_to_all | solution.py:51
  335.9 4.1 copy.59
  340.0 6.3 %copy.60 = bf16[16,256,16,4]{1,3,2,0:T(4,128)(2,1)S(1)} copy(bf16[16,256,16,4]{2,0,3,1:T(8,128)(2,1)} %bitcast.54) | data formatting | bytes 1048576 | tf_op jit(solution)/shard_map/convert_element_type | solution.py:54
  346.4 9.0 %fusion.21 = f32[64,1536]{1,0:T(8,128)} fusion(bf16[16,256,64]{1,2,0:T(8,128)(2,1)S(1)} %convert_element_type.47, bf16[16,256,1536]{2,1,0:T(8,128)(2,1)} %param.7, f32[16,1536]{1,0:T(8,128)S(1)} %get-tuple-element.28, f32[16,1536]{1,0:T(8,128)S(1)} %get-tuple-element.29, f32[16,256]{1,0:T(8,128)S(1)} %add_rsqrt_fusion, ...), kind=kOutput, calls=%fused_computation.26 | convolution fusion | flops 843055104 | bytes 13729792 | tf_op jit(solution)/shard_map/fto,ftd->od/dot_general | solution.py:56
  355.4 16.9 %fusion.12 = (f32[16,1536]{1,0:T(8,128)S(1)}, f32[16,256]{1,0:T(8,128)S(1)}, f32[16,256]{1,0:T(8,128)S(1)}, f32[16,1536]{1,0:T(8,128)S(1)}, f32[16,256,1536]{2,1,0:T(8,128)}) fusion(bf16[16,256,1536]{2,1,0:T(8,128)(2,1)} %param.7, f32[16,256]{1,0:T(8,128)S(1)} %add_rsqrt_fusion, f32[16,256]{1,0:T(8,128)S(1)} %broadcast_multiply_fusion.2, ...), kind=kOutput, calls=%fused_computation.16 | convolution fusion | flops 868163584 | bytes 38830080 | tf_op jit(solution)/shard_map/fto,od->ftd/dot_general | solution.py:55
  372.3 0.7 pad_maximum_fusion
  373.1 0.5 all-reduce.3.cloned.1.call-update
  373.6 18.7 %fusion.11 = bf16[16,256,1536]{2,1,0:T(8,128)(2,1)} fusion(bf16[16,256,1536]{2,1,0:T(8,128)(2,1)} %param.7, f32[16,256,1536]{2,1,0:T(8,128)} %get-tuple-element.27, f32[16,256]{1,0:T(8,128)S(1)} %broadcast_multiply_fusion, f32[16,256]{1,0:T(8,128)S(1)} %broadcast_multiply_fusion.1, f32[16,1536]{1,0:T(8,128)S(1)} %get-tuple-element.29, ...), kind=kLoop, calls=%fused_computation.15 | loop fusion | flops 56623104 | bytes 50495488 | tf_op jit(solution)/shard_map/convert_element_type | solution.py:66
  392.3 9.5 %all-reduce.5.cloned.1.call-done = f32[16,2,1536]{2,0,1:T(8,128)} async-done(((f32[16,2,1536]{2,0,1:T(8,128)}), f32[16,2,1536]{2,0,1:T(8,128)}) %all-reduce.5.cloned.1.call-update) | async-done | bytes 196624 | tf_op jit(solution)/shard_map/psum | solution.py:59
  401.8 1.8 copy.61
  403.6 132.0 %all-reduce.3.cloned.1.call-done = f32[64,1536]{1,0:T(8,128)} async-done(((f32[64,1536]{1,0:T(8,128)}), f32[64,1536]{1,0:T(8,128)}) %all-reduce.3.cloned.1.call-update) | async-done | bytes 393232 | tf_op jit(solution)/shard_map/psum | solution.py:58
  535.6 1.8 copy.75
  (31 shorter events, 1.1 us)
Async XLA Ops:
  7.2 14.7 %copy-start = (bf16[64,1536]{1,0:T(8,128)(2,1)S(1)}, bf16[64,1536]{1,0:T(8,128)(2,1)}, u32[]{:S(2)}) copy-start(bf16[64,1536]{1,0:T(8,128)(2,1)} %param.9) | copy-start | bytes 589828
  7.2 14.5 %copy-start.1 = (f32[16,2,1536]{2,1,0:T(2,128)S(1)}, f32[16,2,1536]{2,1,0:T(2,128)}, u32[]{:S(2)}) copy-start(f32[16,2,1536]{2,1,0:T(2,128)} %param.8) | copy-start | bytes 589828
  7.2 60.1 %all-gather.2.cloned.1.call-start = ((), (), s32[]{:S(2)}) async-start(), calls=%async_computation.4 | async-start | bytes 2621440 | tf_op jit(solution)/shard_map/all_gather | solution.py:29
  42.1 65.4 %copy-start.2 = (s32[8]{0:T(128)S(1)}, s32[8]{0:T(128)}, u32[]{:S(2)}) copy-start(s32[8]{0:T(128)} %param.12) | copy-start | bytes 100
  102.2 53.1 %all-to-all-start = ((bf16[8,2,65536]{2,1,0:T(2,128)(2,1)}), bf16[8,2,65536]{2,1,0:T(2,128)(2,1)S(1)}, u32[]{:S(2)}, u32[]{:S(2)}) async-start(bf16[8,2,65536]{2,1,0:T(2,128)(2,1)} %reshape.137), calls=%async_computation | async-start | bytes 4194304 | tf_op jit(solution)/shard_map/all_to_all | solution.py:30
  107.5 180.5 %reduce-scatter.2.cloned.1.call-start = ((), (), s32[]{:S(2)}) async-start(), calls=%async_computation.5 | async-start | bytes 5242880 | tf_op jit(solution)/shard_map/reduce_scatter | solution.py:46
  168.4 38.8 %copy-start.3 = (s32[8]{0:T(128)S(1)}, s32[8]{0:T(128)}, u32[]{:S(2)}) copy-start(s32[8]{0:T(128)} %param.13) | copy-start | bytes 100
  243.4 158.4 %all-reduce.5.cloned.1.call-start = ((), (), s32[]{:S(2)}) async-start(), calls=%async_computation.7 | async-start | bytes 393216 | tf_op jit(solution)/shard_map/psum | solution.py:59
  373.0 162.6 %all-reduce.3.cloned.1.call-start = ((), (), s32[]{:S(2)}) async-start(), calls=%async_computation.6 | async-start | bytes 786432 | tf_op jit(solution)/shard_map/psum | solution.py:58
Sparse Core Ops, SparseCore 0:
  42.2 25.0 all-gather.1
  243.5 44.4 reduce-scatter.1
  373.1 28.6 all-reduce.4
  407.6 127.9 all-reduce.2
where the time goes:
time: 547 us; the launch traced here: 544 us
  waiting for transfers between devices  259 us (47%)
  local copies, waits for them, and re-layouts  95.2 us (17%)
  other arithmetic  71.4 us (13%)
  blocking collectives  64.4 us (12%)
  matrix products  34.3 us (6%)
  between operations  13.9 us (3%)
    psum x1, waiting for transfers between devices, per_device(): head_grad = lax.psum(head_part, ('tm', 'eval'))  132 us
    all_to_all x1, waiting for transfers between devices, per_device(): lax.all_to_all(frame_whole, 'tm', split_axis=2, concat_axis=0, tiled=True)  47.5 us
    reduce_scatter x1, waiting for transfers between devices, per_device(): lax.psum_scatter(group_grad, 'eval', scatter_dimension=2, tiled=True)  44.5 us
    unnamed x12, local copies, waits for them, and re-layouts  36.2 us
    all_to_all x1, blocking collectives, per_device(): lax.all_to_all(reduced, 'tm', split_axis=0, concat_axis=2, tiled=True)  30.2 us
    scatter-add x1, other arithmetic, per_device(): group_grad = jnp.zeros(latent_all.shape, jnp.float32).at[frame_index.resh...  27.3 us
    all_gather x1, waiting for transfers between devices, per_device(): frame_whole = lax.all_gather(latent, 'eval', axis=2, tiled=True)  25.2 us
    convert_element_type x1, other arithmetic, per_device(): return (d_hidden.astype(jnp.bfloat16), head_grad, mod_grad)  18.7 us
  transfers between devices with their start and end apart: 5, of which 5 were waited for; matrix products, arithmetic and copies ran while one was open for 4% of the time, Pallas kernels for 0%

commit v1 on v0

v1 whole, which is shorter than its diff:
```python
import functools

import jax
import jax.numpy as jnp
from jax import lax
from jax.experimental import pallas as pl
from jax.experimental.pallas import tpu as pltpu
from jax.sharding import PartitionSpec as P

C = 16
PATCH = 4
WIN = 21
TOK = 1024
EPS = 1e-06
LANES = 128
ROWS = 16
MESH = pl.DeviceIdType.MESH
VMEM_LIMIT = 56 * 1024 * 1024
F32 = jnp.float32
BF16 = jnp.bfloat16


def remote(src, dst, send_sem, recv_sem, device):
    return pltpu.make_async_remote_copy(
        src_ref=src, dst_ref=dst, send_sem=send_sem, recv_sem=recv_sem, device_id=device, device_id_type=MESH
    )


def greet(device):
    pl.semaphore_signal(pltpu.get_barrier_semaphore(), inc=1, device_id=device, device_id_type=MESH)


def when_not(flag, action):
    pl.when(jnp.logical_not(flag))(action)


def pixel_permutation(inverse):
    size = PATCH * LANES
    lane = lax.broadcasted_iota(jnp.int32, (size, size), 1 if inverse else 0)
    pixel = lax.broadcasted_iota(jnp.int32, (size, size), 0 if inverse else 1)
    return jnp.where(pixel == (lane & (LANES - 1)) * PATCH + (lane >> 7), 1.0, 0.0).astype(BF16)


def row_permutation(inverse):
    size = C * PATCH
    grouped = lax.broadcasted_iota(jnp.int32, (size, size), 1 if inverse else 0)
    mixed = lax.broadcasted_iota(jnp.int32, (size, size), 0 if inverse else 1)
    return jnp.where(mixed == (grouped & (C - 1)) * PATCH + (grouped >> 4), 1.0, 0.0).astype(BF16)


def dot(a, b, dims=((1,), (0,))):
    return lax.dot_general(a, b, (dims, ((), ())), preferred_element_type=F32)


def forward_kernel(
    n_tm, n_eval, n_blk, starts, hidden, modulation, weight, real, totals, stats,
    adapted, perm, rows, mine, latent, sums, out_send, out_recv, x_send, x_recv, c_send, c_recv, s_send, s_recv,
):
    frame = pl.program_id(0)
    frames = pl.num_programs(0)
    fd = mine.shape[0]
    last = fd - 1
    t = lax.axis_index("tm")
    e = lax.axis_index("eval")
    n_x = n_eval // 2
    x, core = e // 2, e % 2
    partner = 2 * x + 1 - core
    per = fd // n_eval
    tok, width = hidden.shape[1], hidden.shape[2]
    n_win = real.shape[0]

    @pl.when(frame == 0)
    def _():
        source = t // n_blk
        for other in range(n_tm):
            when_not((other == t) & (source == e), lambda: greet((other, source)))
            when_not(other == t, lambda: greet((other, e)))
        for other in range(n_eval):
            when_not(other == e, lambda: greet((t, other)))
        own = jnp.where(source == e, 1, 0)
        pl.semaphore_wait(pltpu.get_barrier_semaphore(), n_tm - own + n_tm - 1 + n_eval - 1)
        perm[...] = pixel_permutation(False)
        rows[...] = row_permutation(False)

    shift = modulation[0, 0:1, :]
    scale = 1.0 + modulation[0, 1:2, :]
    lane = lax.broadcasted_iota(jnp.int32, (ROWS, LANES), 1)

    def chunk(i, carry):
        at = pl.ds(pl.multiple_of(i * ROWS, ROWS), ROWS)
        values = hidden[0, at, :].astype(F32)
        center = jnp.sum(values, axis=1, keepdims=True) * (1.0 / width)
        shifted = values - center
        inv_std = lax.rsqrt(jnp.sum(shifted * shifted, axis=1, keepdims=True) * (1.0 / width) + EPS)
        adapted[at, :] = (shifted * inv_std * scale + shift).astype(BF16)
        stats[0, at, :] = jnp.where(lane == 0, center, inv_std)
        return carry

    lax.fori_loop(0, tok // ROWS, chunk, 0, unroll=2)
    out = dot(weight[...], adapted[...], ((1,), (1,))).astype(BF16)
    grouped = dot(rows[...], out).astype(BF16)
    pixels = []
    for j in range(tok // LANES):
        tile = grouped[:, j * LANES : (j + 1) * LANES]
        wide = jnp.concatenate([tile[s * C : (s + 1) * C] for s in range(PATCH)], axis=1)
        pixels.append(dot(wide, perm[...]).astype(BF16))
    pixels = jnp.concatenate(pixels, axis=1)
    pixel_block = mine.shape[3]
    target = frame % n_eval
    place = frame // n_eval
    for b in range(n_blk):
        mine[frame, b] = pixels[:, b * pixel_block : (b + 1) * pixel_block]
    for b in range(n_blk):
        owner = e * n_blk + b
        own = (owner == t) & (target == e)
        dst = latent.at[target, place, t]

        @pl.when(own)
        def _():
            pltpu.make_async_copy(mine.at[frame, b], dst, out_recv.at[place, t]).start()

        @pl.when(jnp.logical_not(own))
        def _():
            remote(mine.at[frame, b], dst, out_send.at[frame, b], out_recv.at[place, t], (owner, target)).start()

    def x_copy(r, d):
        there = 2 * ((x + d) % n_x) + core
        return remote(latent.at[e, r], latent.at[e, r], x_send.at[r, d - 1], x_recv.at[r, d - 1], (t, there))

    def core_copy(r, d):
        held = 2 * ((x + n_x - d) % n_x) + core
        return remote(latent.at[held, r], latent.at[held, r], c_send.at[r, d], c_recv.at[r, d], (t, partner))

    def first(r):
        for source in range(n_tm):
            pltpu.make_async_copy(mine.at[0, 0], latent.at[e, r, source], out_recv.at[r, source]).wait()
        for d in range(1, n_x):
            x_copy(r, d).start()
        core_copy(r, 0).start()

    def second(r):
        for d in range(1, n_x):
            x_copy(r, d).wait_recv()
            core_copy(r, d).start()

    for r in range(per):
        pl.when(frame == min((r + 2) * n_eval - 1, last))(functools.partial(first, r))
    for r in range(per):
        pl.when(frame == min((r + 3) * n_eval - 1, last))(functools.partial(second, r))

    @pl.when(frame == frames - 1)
    def _():
        for f in range(fd):
            for b in range(n_blk):
                owner = e * n_blk + b
                own = (owner == t) & (f % n_eval == e)
                when_not(
                    own,
                    lambda: remote(
                        mine.at[f, b], mine.at[f, b], out_send.at[f, b], out_recv.at[0, 0], (owner, f % n_eval)
                    ).wait_send(),
                )
        for r in range(per):
            for d in range(1, n_x):
                x_copy(r, d).wait_send()
            for d in range(n_x):
                core_copy(r, d).wait()
        row = lax.broadcasted_iota(jnp.int32, (n_win, LANES), 0)
        found = jnp.zeros((n_win, LANES), F32)
        for w in range(n_win):
            start = starts[w]

            def add(k, acc):
                g = start + k
                inner = g % fd
                block = latent[inner % n_eval, inner // n_eval, g // fd].astype(F32)
                return acc + jnp.abs(block - real[w, k].astype(F32))

            acc = lax.fori_loop(0, WIN, add, jnp.zeros(real.shape[2:], F32), unroll=3)
            total = jnp.sum(jnp.sum(acc, axis=0, keepdims=True), axis=1, keepdims=True)
            found = jnp.where(row == w, total, found)
        sums[t] = found
        for d in range(1, n_tm):
            there = (t + d) % n_tm
            remote(sums.at[t], sums.at[t], s_send.at[d - 1], s_recv.at[d - 1], (there, e)).start()
        for d in range(1, n_tm):
            origin = (t + n_tm - d) % n_tm
            remote(sums.at[origin], sums.at[origin], s_send.at[d - 1], s_recv.at[d - 1], (origin, e)).wait()
        result = sums[0]
        for other in range(1, n_tm):
            result = result + sums[other]
        totals[...] = result


def window_kernel(n_pixels, starts, totals, times, real, fake, out):
    out[...] = jnp.zeros_like(out)
    level = times[...].astype(F32) / 1000.0 / (totals[...] / n_pixels + 1e-05)
    for w in range(real.shape[0]):
        start = starts[w]
        gain = level[w : w + 1, 0:1]

        def add(k, carry):
            out[start + k] += gain * (fake[w, k].astype(F32) - real[w, k].astype(F32))
            return carry

        lax.fori_loop(0, WIN, add, 0, unroll=3)


def reduce_kernel(
    n_tm, n_eval, n_blk, grad, out,
    from_core, half, from_x, rounded, landed, c_send, c_recv, x_send, x_recv, o_send, o_recv,
):
    t = lax.axis_index("tm")
    e = lax.axis_index("eval")
    n_x = n_eval // 2
    x, core = e // 2, e % 2
    partner = 2 * x + 1 - core
    fd = grad.shape[1]
    per = fd // n_eval
    mid = fd // 2
    home = t // n_blk
    slot = t % n_blk
    quarter = core * n_x + x

    for other in range(n_eval):
        when_not(other == e, lambda: greet((t, other)))
        for b in range(n_blk):
            when_not((e * n_blk + b == t) & (other == e), lambda: greet((e * n_blk + b, other)))
    own_home = jnp.where(home == e, 1, 0)
    pl.semaphore_wait(pltpu.get_barrier_semaphore(), n_eval - 1 + n_tm - own_home)

    def core_copy(o):
        return remote(
            grad.at[o, pl.ds((1 - core) * mid, mid)], from_core.at[o], c_send.at[o], c_recv.at[o], (t, partner)
        )

    def x_copy(o, d):
        there = (x + d) % n_x
        return remote(
            half.at[o, pl.ds(there * per, per)], from_x.at[o, d - 1], x_send.at[o, d - 1], x_recv.at[o, d - 1],
            (t, 2 * there + core),
        )

    def out_copy(o):
        return remote(
            rounded.at[o], landed.at[slot, quarter], o_send.at[o], o_recv.at[slot, quarter], (o, home)
        )

    def order(i):
        return (t + i) % n_tm

    def start_core(i, carry):
        core_copy(order(i)).start()
        return carry

    def combine(i, carry):
        o = order(i)
        core_copy(o).wait_recv()
        half[o] = grad[o, pl.ds(core * mid, mid)] + from_core[o]
        for d in range(1, n_x):
            x_copy(o, d).start()
        return carry

    def finish(i, carry):
        o = order(i)
        total = half[o, pl.ds(x * per, per)]
        for d in range(1, n_x):
            x_copy(o, d).wait_recv()
            total = total + from_x[o, d - 1]
        rounded[o] = total.astype(BF16)
        own = (o == t) & (home == e)

        @pl.when(own)
        def _():
            pltpu.make_async_copy(rounded.at[o], landed.at[slot, quarter], o_recv.at[slot, quarter]).start()

        @pl.when(jnp.logical_not(own))
        def _():
            out_copy(o).start()

        return carry

    def drain(i, carry):
        o = order(i)
        core_copy(o).wait_send()
        for d in range(1, n_x):
            x_copy(o, d).wait_send()
        when_not((o == t) & (home == e), lambda: out_copy(o).wait_send())
        return carry

    lax.fori_loop(0, n_tm, start_core, 0)
    lax.fori_loop(0, n_tm, combine, 0)
    lax.fori_loop(0, n_tm, finish, 0)
    lax.fori_loop(0, n_tm, drain, 0)
    for b in range(n_blk):
        for q in range(n_eval):
            pltpu.make_async_copy(rounded.at[0], landed.at[b, q], o_recv.at[b, q]).wait()
    pixel_block = grad.shape[3]
    for b in range(n_blk):
        out[:, :, b * pixel_block : (b + 1) * pixel_block] = landed[b].reshape(fd, C, pixel_block)


def backward_kernel(
    hidden, modulation, weight, stats, upstream, d_hidden, head_part, mod_part,
    adapted, d_adapted, perm, rows, sum_a, sum_b,
):
    frame = pl.program_id(0)
    tok, width = hidden.shape[1], hidden.shape[2]

    @pl.when(frame == 0)
    def _():
        perm[...] = pixel_permutation(True)
        rows[...] = row_permutation(True)
        head_part[...] = jnp.zeros_like(head_part)

    shift = modulation[0, 0:1, :]
    scale = 1.0 + modulation[0, 1:2, :]
    size = LANES * PATCH
    tiles = []
    for j in range(tok // LANES):
        wide = dot(upstream[0, :, j * size : (j + 1) * size], perm[...]).astype(BF16)
        tiles.append(jnp.concatenate([wide[:, s * LANES : (s + 1) * LANES] for s in range(PATCH)], axis=0))
    up = dot(rows[...], jnp.concatenate(tiles, axis=1)).astype(BF16)
    d_adapted[...] = dot(up, weight[...], ((0,), (0,)))
    sum_a[...] = jnp.zeros_like(sum_a)
    sum_b[...] = jnp.zeros_like(sum_b)

    def chunk(i, carry):
        at = pl.ds(pl.multiple_of(i * ROWS, ROWS), ROWS)
        center = stats[0, at, 0:1]
        inv_std = stats[0, at, 1:2]
        normed = (hidden[0, at, :].astype(F32) - center) * inv_std
        adapted[at, :] = (normed * scale + shift).astype(BF16)
        da = d_adapted[at, :]
        cross = da * normed
        sum_a[...] += da[0:8] + da[8:16]
        sum_b[...] += cross[0:8] + cross[8:16]
        dn = da * scale
        mean_a = jnp.sum(dn, axis=1, keepdims=True) * (1.0 / width)
        mean_b = jnp.sum(cross * scale, axis=1, keepdims=True) * (1.0 / width)
        d_hidden[0, at, :] = (inv_std * (dn - mean_a - normed * mean_b)).astype(BF16)
        return carry

    lax.fori_loop(0, tok // ROWS, chunk, 0, unroll=2)
    head_part[...] += dot(up, adapted[...])
    mod_part[0, 0:1, :] = jnp.sum(sum_a[...], axis=0, keepdims=True)
    mod_part[0, 1:2, :] = jnp.sum(sum_b[...], axis=0, keepdims=True)


def sum_kernel(
    n_tm, n_eval, head, mod, head_out, mod_out,
    from_eval, from_tm, mod_in, a_send, a_recv, b_send, b_recv, g_send, g_recv, h_send, h_recv, m_send, m_recv,
    k_send, k_recv, head_all, mod_all, mine,
):
    t = lax.axis_index("tm")
    e = lax.axis_index("eval")
    for other in range(n_eval):
        when_not(other == e, lambda: greet((t, other)))
    for other in range(n_tm):
        when_not(other == t, lambda: greet((other, e)))
    pl.semaphore_wait(pltpu.get_barrier_semaphore(), n_eval - 1 + n_tm - 1)

    def eval_peer(d):
        return (e + d) % n_eval

    def tm_peer(d):
        return (t + d) % n_tm

    def head_in(d):
        return remote(head.at[eval_peer(d)], from_eval.at[d - 1], a_send.at[d - 1], a_recv.at[d - 1], (t, eval_peer(d)))

    def mod_scatter(d):
        return remote(mod.at[eval_peer(d)], mod_in.at[d - 1], m_send.at[d - 1], m_recv.at[d - 1], (t, eval_peer(d)))

    for d in range(1, n_eval):
        head_in(d).start()
    for d in range(1, n_eval):
        mod_scatter(d).start()
    part = head[e]
    for d in range(1, n_eval):
        head_in(d).wait_recv()
        part = part + from_eval[d - 1]
    mine[...] = part

    def tm_in(d):
        return remote(mine.at[tm_peer(d)], from_tm.at[d - 1], b_send.at[d - 1], b_recv.at[d - 1], (tm_peer(d), e))

    for d in range(1, n_tm):
        tm_in(d).start()
    mod_sum = mod[e]
    for d in range(1, n_eval):
        mod_scatter(d).wait_recv()
        mod_sum = mod_sum + mod_in[d - 1]
    mod_all[e] = mod_sum

    def mod_spread(d):
        return remote(mod_all.at[e], mod_all.at[e], k_send.at[d - 1], k_recv.at[d - 1], (t, eval_peer(d)))

    for d in range(1, n_eval):
        mod_spread(d).start()
    total = mine[t]
    for d in range(1, n_tm):
        tm_in(d).wait_recv()
        total = total + from_tm[d - 1]
    head_all[e, t] = total

    def tm_spread(d):
        return remote(head_all.at[e, t], head_all.at[e, t], g_send.at[d - 1], g_recv.at[d - 1], (tm_peer(d), e))

    def eval_spread(d):
        return remote(head_all.at[e], head_all.at[e], h_send.at[d - 1], h_recv.at[d - 1], (t, eval_peer(d)))

    for d in range(1, n_tm):
        tm_spread(d).start()
    for d in range(1, n_tm):
        tm_spread(d).wait()
    for d in range(1, n_eval):
        eval_spread(d).start()
    for d in range(1, n_eval):
        head_in(d).wait_send()
        mod_scatter(d).wait_send()
        mod_spread(d).wait()
    for d in range(1, n_tm):
        tm_in(d).wait_send()
    mod_out[...] = mod_all[...]
    for d in range(1, n_eval):
        eval_spread(d).wait()
    head_out[...] = head_all[...]


def params(collective=None):
    if collective is None:
        return pltpu.CompilerParams(vmem_limit_bytes=VMEM_LIMIT)
    return pltpu.CompilerParams(vmem_limit_bytes=VMEM_LIMIT, collective_id=collective, has_side_effects=True)


def per_device(hidden, modulation, head_weight, real_score, fake_score, window_start, timestep):
    fd, tok, width = hidden.shape
    n_tm = lax.axis_size("tm")
    n_eval = lax.axis_size("eval")
    n_win = real_score.shape[0]
    pixel_block = real_score.shape[3]
    n_blk = tok * PATCH // pixel_block
    per = fd // n_eval
    n_x = n_eval // 2
    size = LANES * PATCH
    dma = pltpu.SemaphoreType.DMA
    vmem = pl.BlockSpec(memory_space=pltpu.VMEM)
    smem = pl.BlockSpec(memory_space=pltpu.SMEM)
    by_frame = pl.BlockSpec((1, tok, width), lambda f: (f, 0, 0))
    mod_frame = pl.BlockSpec((1, 2, width), lambda f: (f, 0, 0))
    stat_frame = pl.BlockSpec((1, tok, LANES), lambda f: (f, 0, 0))
    extra_x = max(n_x - 1, 1)

    totals, stats = pl.pallas_call(
        functools.partial(forward_kernel, n_tm, n_eval, n_blk),
        grid=(fd,),
        out_shape=(
            jax.ShapeDtypeStruct((n_win, LANES), F32),
            jax.ShapeDtypeStruct((fd, tok, LANES), F32),
        ),
        in_specs=[smem, by_frame, mod_frame, vmem, vmem],
        out_specs=(pl.BlockSpec((n_win, LANES), lambda f: (0, 0)), stat_frame),
        scratch_shapes=[
            pltpu.VMEM((tok, width), BF16),
            pltpu.VMEM((size, size), BF16),
            pltpu.VMEM((C * PATCH, C * PATCH), BF16),
            pltpu.VMEM((fd, n_blk, C, pixel_block), BF16),
            pltpu.VMEM((n_eval, per, n_tm, C, pixel_block), BF16),
            pltpu.VMEM((n_tm, n_win, LANES), F32),
            dma((fd, n_blk)),
            dma((per, n_tm)),
            dma((per, extra_x)),
            dma((per, extra_x)),
            dma((per, n_x)),
            dma((per, n_x)),
            dma((n_tm - 1,)),
            dma((n_tm - 1,)),
        ],
        compiler_params=params(0),
        name="forward",
    )(window_start, hidden, modulation, head_weight, real_score)

    frames = fd * n_tm
    grad = pl.pallas_call(
        functools.partial(window_kernel, float(WIN * C * pixel_block * n_tm)),
        out_shape=jax.ShapeDtypeStruct((frames, C, pixel_block), F32),
        in_specs=[smem, vmem, vmem, vmem, vmem],
        out_specs=vmem,
        compiler_params=params(),
        name="windows",
    )(window_start, totals, jnp.broadcast_to(timestep[:, None], (n_win, LANES)), real_score, fake_score)

    upstream = pl.pallas_call(
        functools.partial(reduce_kernel, n_tm, n_eval, n_blk),
        out_shape=jax.ShapeDtypeStruct((fd, C, tok * PATCH), BF16),
        in_specs=[vmem],
        out_specs=vmem,
        scratch_shapes=[
            pltpu.VMEM((n_tm, fd // 2, C, pixel_block), F32),
            pltpu.VMEM((n_tm, fd // 2, C, pixel_block), F32),
            pltpu.VMEM((n_tm, extra_x, per, C, pixel_block), F32),
            pltpu.VMEM((n_tm, per, C, pixel_block), BF16),
            pltpu.VMEM((n_blk, n_eval, per, C, pixel_block), BF16),
            dma((n_tm,)),
            dma((n_tm,)),
            dma((n_tm, extra_x)),
            dma((n_tm, extra_x)),
            dma((n_tm,)),
            dma((n_blk, n_eval)),
        ],
        compiler_params=params(1),
        name="reduce",
    )(grad.reshape(n_tm, fd, C, pixel_block))

    d_hidden, head_part, mod_part = pl.pallas_call(
        backward_kernel,
        grid=(fd,),
        out_shape=(
            jax.ShapeDtypeStruct(hidden.shape, BF16),
            jax.ShapeDtypeStruct(head_weight.shape, F32),
            jax.ShapeDtypeStruct((fd, 2, width), F32),
        ),
        in_specs=[
            by_frame,
            mod_frame,
            vmem,
            stat_frame,
            pl.BlockSpec((1, C, tok * PATCH), lambda f: (f, 0, 0)),
        ],
        out_specs=(by_frame, pl.BlockSpec(head_weight.shape, lambda f: (0, 0)), mod_frame),
        scratch_shapes=[
            pltpu.VMEM((tok, width), BF16),
            pltpu.VMEM((tok, width), F32),
            pltpu.VMEM((size, size), BF16),
            pltpu.VMEM((C * PATCH, C * PATCH), BF16),
            pltpu.VMEM((8, width), F32),
            pltpu.VMEM((8, width), F32),
        ],
        compiler_params=params(),
        name="backward",
    )(hidden, modulation, head_weight, stats, upstream)

    head_rows = head_part.size // (n_tm * n_eval * LANES)
    mod_rows = mod_part.size // (n_eval * LANES)
    head_shape = (n_eval, n_tm, head_rows, LANES)
    mod_shape = (n_eval, mod_rows, LANES)
    e_sem, t_sem = dma((n_eval - 1,)), dma((n_tm - 1,))
    head_grad, mod_grad = pl.pallas_call(
        functools.partial(sum_kernel, n_tm, n_eval),
        out_shape=(jax.ShapeDtypeStruct(head_shape, F32), jax.ShapeDtypeStruct(mod_shape, F32)),
        in_specs=[vmem, vmem],
        out_specs=(vmem, vmem),
        scratch_shapes=[
            pltpu.VMEM((n_eval - 1,) + head_shape[1:], F32),
            pltpu.VMEM((n_tm - 1,) + head_shape[2:], F32),
            pltpu.VMEM((n_eval - 1,) + mod_shape[1:], F32),
            e_sem, e_sem, t_sem, t_sem, t_sem, t_sem, e_sem, e_sem, e_sem, e_sem, e_sem, e_sem,
            pltpu.VMEM(head_shape, F32),
            pltpu.VMEM(mod_shape, F32),
            pltpu.VMEM(head_shape[1:], F32),
        ],
        compiler_params=params(2),
        name="sums",
    )(head_part.reshape(head_shape), mod_part.reshape(mod_shape))
    return (d_hidden, head_grad.reshape(head_part.shape), mod_grad.reshape(mod_part.shape))


def solution(mesh):
    placed = (
        P("tm", "eval", None),
        P("tm", None, None),
        P(),
        P("eval", None, None, "tm"),
        P("eval", None, None, "tm"),
        P("eval"),
        P("eval"),
    )
    return jax.shard_map(
        per_device,
        mesh=mesh,
        in_specs=placed,
        out_specs=(P("tm", "eval", None), P(), P("tm", None, None)),
        check_vma=False,
    )
```

time: 547 us -> 199 us (0.36)
  waiting for transfers between devices: 259 us -> 0 us
  Pallas kernels: 0 us -> 190 us
  local copies, waits for them, and re-layouts: 95.2 us -> 8.38 us
  other arithmetic: 71.4 us -> 0 us
  blocking collectives: 64.4 us -> 0 us
  matrix products: 34.3 us -> 0 us
  between operations: 13.9 us -> 0.66 us
    pallas_call x0 -> x5, Pallas kernels: none -> 190 us  [the longest x1 67.9 us: per_device(): pl.pallas_call(functools.partial(forward_kernel, n_tm, n_eval, n_blk), gr...]
    psum x2 -> x0, waiting for transfers between devices: 142 us -> none  [the longest x1 132 us: per_device(): head_grad = lax.psum(head_part, ('tm', 'eval'))]
    all_to_all x2 -> x0, blocking collectives: 47.8 us -> none  [the longest x1 30.2 us: per_device(): lax.all_to_all(reduced, 'tm', split_axis=0, concat_axis=2, tiled=True)]
    all_to_all x1 -> x0, waiting for transfers between devices: 47.5 us -> none  [per_device(): lax.all_to_all(frame_whole, 'tm', split_axis=2, concat_axis=0, tiled=True)]
    reduce_scatter x1 -> x0, waiting for transfers between devices: 44.5 us -> none  [per_device(): lax.psum_scatter(group_grad, 'eval', scatter_dimension=2, tiled=True)]
    unnamed x12 -> x0, local copies, waits for them, and re-layouts: 36.2 us -> none
    dot_general x3 -> x0, matrix products: 34.3 us -> none  [the longest x1 16.9 us: per_device(): jnp.einsum('fto,od->ftd', upstream, head_weight, preferred_element_type=j...]
    scatter-add x1 -> x0, other arithmetic: 27.3 us -> none  [per_device(): group_grad = jnp.zeros(latent_all.shape, jnp.float32).at[frame_index.resh...]
  transfers between devices with their start and end apart: 5 -> 0, of which waited for: 5 -> 0; matrix products, arithmetic and copies ran while one was open for 4% -> 0% of each run, Pallas kernels for 0% -> 0%
where the time goes in v1:
time: 199 us
  Pallas kernels  190 us (95%)
  local copies, waits for them, and re-layouts  8.38 us (4%)
    pallas_call x1, Pallas kernels, per_device(): pl.pallas_call(functools.partial(forward_kernel, n_tm, n_eval, n_blk), gr...  67.9 us
    pallas_call x1, Pallas kernels, per_device(): pl.pallas_call(backward_kernel, grid=(fd,), out_shape=(jax.ShapeDtypeStru...  47.5 us
    pallas_call x1, Pallas kernels, per_device(): pl.pallas_call(functools.partial(reduce_kernel, n_tm, n_eval, n_blk), out...  37.3 us
    pallas_call x1, Pallas kernels, per_device(): pl.pallas_call(functools.partial(sum_kernel, n_tm, n_eval), out_shape=(ja...  29.6 us
    pallas_call x1, Pallas kernels, per_device(): pl.pallas_call(functools.partial(window_kernel, float(WIN * C * pixel_blo...  7.39 us

profile of v1, /device:TPU:1, one launch (start us, length us, event | category | flops | bytes accessed | tf_op | source)
XLA Modules:
  0.0 198.7 jit_solution(14889136768444433996)
XLA Ops:
  0.6 1.3 broadcast_in_dim.2.times
  1.9 67.9 %forward.1 = (f32[8,128]{1,0:T(8,128)}, f32[16,256,128]{2,1,0:T(8,128)}) custom-call(s32[8]{0:T(128)} %starts.3, bf16[16,256,1536]{2,1,0:T(8,128)(2,1)} %hidden.3, f32[16,2,1536]{2,1,0:T(2,128)} %modulation.3, bf16[64,1536]{1,0:T(8,128)(2,1)} %weight.3, bf16[8,21,16,512]{3,2,1,0:T(8,128)(2,1)} %real.3), custom_call_target="tpu_custom_call" | custom-call | tf_op jit(solution)/shard_map/forward/pallas_call | solution.py:455
  69.8 7.4 %windows.1 = f32[128,16,512]{2,1,0:T(8,128)} custom-call(s32[8]{0:T(128)} %starts.3, f32[8,128]{1,0:T(8,128)} %get-tuple-element.11.totals, s32[8,128]{1,0:T(8,128)} %broadcast_in_dim.2.times, bf16[8,21,16,512]{3,2,1,0:T(8,128)(2,1)} %real.3, bf16[8,21,16,512]{3,2,1,0:T(8,128)(2,1)} %fake.1), custom_call_target="tpu_custom_call" | custom-call | tf_op jit(solution)/shard_map/windows/pallas_call | solution.py:485
  77.2 37.3 %reduce.1.upstream = bf16[16,16,1024]{2,1,0:T(8,128)(2,1)} custom-call(f32[8,16,16,512]{3,2,1,0:T(8,128)} %bitcast.3), custom_call_target="tpu_custom_call" | custom-call | tf_op jit(solution)/shard_map/reduce/pallas_call | solution.py:494
  114.6 47.5 %backward.1 = (bf16[16,256,1536]{2,1,0:T(8,128)(2,1)}, f32[64,1536]{1,0:T(8,128)}, f32[16,2,1536]{2,1,0:T(2,128)}) custom-call(bf16[16,256,1536]{2,1,0:T(8,128)(2,1)} %hidden.3, f32[16,2,1536]{2,1,0:T(2,128)} %modulation.3, bf16[64,1536]{1,0:T(8,128)(2,1)} %weight.3, f32[16,256,128]{2,1,0:T(8,128)} %get-tuple-element.10.stats, ...), custom_call_target="tpu_custom_call" | custom-call | tf_op jit(solution)/shard_map/backward/pallas_call | solution.py:516
  162.1 1.8 reshape.24.mod
  163.9 1.8 reshape.23.head
  165.6 29.6 %sums.1 = (f32[4,8,24,128]{3,2,1,0:T(8,128)}, f32[4,96,128]{2,1,0:T(8,128)}) custom-call(f32[4,8,24,128]{3,2,1,0:T(8,128)} %reshape.23.head, f32[4,96,128]{2,1,0:T(8,128)} %reshape.24.mod), custom_call_target="tpu_custom_call" | custom-call | tf_op jit(solution)/shard_map/sums/pallas_call | solution.py:549
  195.2 1.8 reshape.25
  197.0 1.7 reshape.26

commit v2 on v1

--- a/solution.py
+++ b/solution.py
@@ -48,13 +48,17 @@
     return jnp.where(mixed == (grouped & (C - 1)) * PATCH + (grouped >> 4), 1.0, 0.0).astype(BF16)
 
 
+def chunk_rows(i):
+    return pl.ds(pl.multiple_of(i * ROWS, ROWS), ROWS)
+
+
 def dot(a, b, dims=((1,), (0,))):
     return lax.dot_general(a, b, (dims, ((), ())), preferred_element_type=F32)
 
 
 def forward_kernel(
-    n_tm, n_eval, n_blk, starts, hidden, modulation, weight, real, totals, stats,
-    adapted, perm, rows, mine, latent, sums, out_send, out_recv, x_send, x_recv, c_send, c_recv, s_send, s_recv,
+    n_tm, n_eval, n_blk, starts, hidden, modulation, weight, real, totals, center, inv_std,
+    adapted, part, perm, rows, mine, latent, sums, out_send, out_recv, x_send, x_recv, c_send, c_recv, s_send, s_recv,
 ):
     frame = pl.program_id(0)
     frames = pl.num_programs(0)
@@ -84,19 +88,35 @@
 
     shift = modulation[0, 0:1, :]
     scale = 1.0 + modulation[0, 1:2, :]
-    lane = lax.broadcasted_iota(jnp.int32, (ROWS, LANES), 1)
-
-    def chunk(i, carry):
-        at = pl.ds(pl.multiple_of(i * ROWS, ROWS), ROWS)
-        values = hidden[0, at, :].astype(F32)
-        center = jnp.sum(values, axis=1, keepdims=True) * (1.0 / width)
-        shifted = values - center
-        inv_std = lax.rsqrt(jnp.sum(shifted * shifted, axis=1, keepdims=True) * (1.0 / width) + EPS)
-        adapted[at, :] = (shifted * inv_std * scale + shift).astype(BF16)
-        stats[0, at, :] = jnp.where(lane == 0, center, inv_std)
+    tiles = [slice(i * LANES, (i + 1) * LANES) for i in range(width // LANES)]
+
+    def row_sums(body):
+        def step(i, carry):
+            at = chunk_rows(i)
+            acc = body(at, tiles[0])
+            for tile in tiles[1:]:
+                acc = acc + body(at, tile)
+            part[at, :] = acc
+            return carry
+
+        lax.fori_loop(0, tok // ROWS, step, 0, unroll=4)
+        return jnp.broadcast_to(jnp.sum(part[...], axis=1, keepdims=True) * (1.0 / width), (tok, LANES))
+
+    def squares(at, tile):
+        shifted = hidden[0, at, tile].astype(F32) - center[0, at, :]
+        return shifted * shifted
+
+    center[0] = row_sums(lambda at, tile: hidden[0, at, tile].astype(F32))
+    inv_std[0] = lax.rsqrt(row_sums(squares) + EPS)
+
+    def adapt(i, carry):
+        at = chunk_rows(i)
+        for tile in tiles:
+            normed = (hidden[0, at, tile].astype(F32) - center[0, at, :]) * inv_std[0, at, :]
+            adapted[at, tile] = (normed * scale[:, tile] + shift[:, tile]).astype(BF16)
         return carry
 
-    lax.fori_loop(0, tok // ROWS, chunk, 0, unroll=2)
+    lax.fori_loop(0, tok // ROWS, adapt, 0, unroll=4)
     out = dot(weight[...], adapted[...], ((1,), (1,))).astype(BF16)
     grouped = dot(rows[...], out).astype(BF16)
     pixels = []
@@ -301,8 +321,8 @@
 
 
 def backward_kernel(
-    hidden, modulation, weight, stats, upstream, d_hidden, head_part, mod_part,
-    adapted, d_adapted, perm, rows, sum_a, sum_b,
+    hidden, modulation, weight, center, inv_std, upstream, d_hidden, head_tiles, mod_part,
+    adapted, d_adapted, perm, rows, head, sum_b, part, mean_a, mean_b,
 ):
     frame = pl.program_id(0)
     tok, width = hidden.shape[1], hidden.shape[2]
@@ -311,40 +331,73 @@
     def _():
         perm[...] = pixel_permutation(True)
         rows[...] = row_permutation(True)
-        head_part[...] = jnp.zeros_like(head_part)
+        head[...] = jnp.zeros_like(head)
 
     shift = modulation[0, 0:1, :]
     scale = 1.0 + modulation[0, 1:2, :]
     size = LANES * PATCH
-    tiles = []
+    blocks = []
     for j in range(tok // LANES):
         wide = dot(upstream[0, :, j * size : (j + 1) * size], perm[...]).astype(BF16)
-        tiles.append(jnp.concatenate([wide[:, s * LANES : (s + 1) * LANES] for s in range(PATCH)], axis=0))
-    up = dot(rows[...], jnp.concatenate(tiles, axis=1)).astype(BF16)
+        blocks.append(jnp.concatenate([wide[:, s * LANES : (s + 1) * LANES] for s in range(PATCH)], axis=0))
+    up = dot(rows[...], jnp.concatenate(blocks, axis=1)).astype(BF16)
     d_adapted[...] = dot(up, weight[...], ((0,), (0,)))
-    sum_a[...] = jnp.zeros_like(sum_a)
+    weight_f32 = weight[...].astype(F32)
+    up_sum = jnp.sum(up.astype(F32), axis=1, keepdims=True)
+    mod_part[0, 0:1, :] = jnp.sum(weight_f32 * up_sum, axis=0, keepdims=True)
+
+    level = jnp.sum(weight_f32 * scale, axis=1, keepdims=True) * (1.0 / width)
+    rest = jnp.broadcast_to(level, (level.shape[0], LANES))
+    total = jnp.zeros((tok, LANES), F32)
+    for _ in range(3):
+        term = rest.astype(BF16)
+        total = total + dot(up, term, ((0,), (0,)))
+        rest = rest - term.astype(F32)
+    mean_a[...] = total * inv_std[0]
     sum_b[...] = jnp.zeros_like(sum_b)
-
-    def chunk(i, carry):
-        at = pl.ds(pl.multiple_of(i * ROWS, ROWS), ROWS)
-        center = stats[0, at, 0:1]
-        inv_std = stats[0, at, 1:2]
-        normed = (hidden[0, at, :].astype(F32) - center) * inv_std
-        adapted[at, :] = (normed * scale + shift).astype(BF16)
-        da = d_adapted[at, :]
-        cross = da * normed
-        sum_a[...] += da[0:8] + da[8:16]
-        sum_b[...] += cross[0:8] + cross[8:16]
-        dn = da * scale
-        mean_a = jnp.sum(dn, axis=1, keepdims=True) * (1.0 / width)
-        mean_b = jnp.sum(cross * scale, axis=1, keepdims=True) * (1.0 / width)
-        d_hidden[0, at, :] = (inv_std * (dn - mean_a - normed * mean_b)).astype(BF16)
+    tiles = [slice(i * LANES, (i + 1) * LANES) for i in range(width // LANES)]
+
+    def gather(i, carry):
+        at = chunk_rows(i)
+        acc = jnp.zeros((ROWS, LANES), F32)
+        for tile in tiles:
+            normed = (hidden[0, at, tile].astype(F32) - center[0, at, :]) * inv_std[0, at, :]
+            scaled = normed * scale[:, tile]
+            adapted[at, tile] = (scaled + shift[:, tile]).astype(BF16)
+            da = d_adapted[at, tile]
+            acc = acc + da * scaled
+            cross = da * normed
+            sum_b[:, tile] += cross[0:8] + cross[8:16]
+        part[at, :] = acc
         return carry
 
-    lax.fori_loop(0, tok // ROWS, chunk, 0, unroll=2)
-    head_part[...] += dot(up, adapted[...])
-    mod_part[0, 0:1, :] = jnp.sum(sum_a[...], axis=0, keepdims=True)
+    lax.fori_loop(0, tok // ROWS, gather, 0, unroll=4)
+    mean_cross = jnp.sum(part[...], axis=1, keepdims=True) * (1.0 / width)
+    mean_b[...] = mean_cross * inv_std[0] * inv_std[0]
+    head[...] += dot(up, adapted[...])
+
+    def finish(i, carry):
+        at = chunk_rows(i)
+        for tile in tiles:
+            shifted = hidden[0, at, tile].astype(F32) - center[0, at, :]
+            dn = d_adapted[at, tile] * scale[:, tile] * inv_std[0, at, :]
+            d_hidden[0, at, tile] = (dn - mean_a[at, :] - shifted * mean_b[at, :]).astype(BF16)
+        return carry
+
+    lax.fori_loop(0, tok // ROWS, finish, 0, unroll=4)
     mod_part[0, 1:2, :] = jnp.sum(sum_b[...], axis=0, keepdims=True)
+
+    @pl.when(frame == pl.num_programs(0) - 1)
+    def _():
+        per = head_tiles.shape[2]
+        n_tm = head_tiles.shape[1]
+        place = 0
+        for tile in tiles:
+            for r in range(0, head.shape[0], 8):
+                head_tiles[place // (per * n_tm), place // per % n_tm, place % per] = head[r : r + 8, tile]
+                place += 1
+        for place in range(place, head_tiles.shape[0] * n_tm * per):
+            head_tiles[place // (per * n_tm), place // per % n_tm, place % per] = jnp.zeros((8, LANES), F32)
 
 
 def sum_kernel(
@@ -425,7 +478,12 @@
     mod_out[...] = mod_all[...]
     for d in range(1, n_eval):
         eval_spread(d).wait()
-    head_out[...] = head_all[...]
+    per = head_all.shape[2]
+    place = 0
+    for col in range(0, head_out.shape[1], LANES):
+        for r in range(0, head_out.shape[0], 8):
+            head_out[r : r + 8, col : col + LANES] = head_all[place // (per * n_tm), place // per % n_tm, place % per]
+            place += 1
 
 
 def params(collective=None):
@@ -452,17 +510,19 @@
     stat_frame = pl.BlockSpec((1, tok, LANES), lambda f: (f, 0, 0))
     extra_x = max(n_x - 1, 1)
 
-    totals, stats = pl.pallas_call(
+    totals, center, inv_std = pl.pallas_call(
         functools.partial(forward_kernel, n_tm, n_eval, n_blk),
         grid=(fd,),
         out_shape=(
             jax.ShapeDtypeStruct((n_win, LANES), F32),
             jax.ShapeDtypeStruct((fd, tok, LANES), F32),
+            jax.ShapeDtypeStruct((fd, tok, LANES), F32),
         ),
         in_specs=[smem, by_frame, mod_frame, vmem, vmem],
-        out_specs=(pl.BlockSpec((n_win, LANES), lambda f: (0, 0)), stat_frame),
+        out_specs=(pl.BlockSpec((n_win, LANES), lambda f: (0, 0)), stat_frame, stat_frame),
         scratch_shapes=[
             pltpu.VMEM((tok, width), BF16),
+            pltpu.VMEM((tok, LANES), F32),
             pltpu.VMEM((size, size), BF16),
             pltpu.VMEM((C * PATCH, C * PATCH), BF16),
             pltpu.VMEM((fd, n_blk, C, pixel_block), BF16),
@@ -513,12 +573,14 @@
         name="reduce",
     )(grad.reshape(n_tm, fd, C, pixel_block))
 
+    head_tiles = width // LANES * (C * PATCH // 8)
+    head_shape = (n_eval, n_tm, pl.cdiv(head_tiles, n_eval * n_tm), 8, LANES)
     d_hidden, head_part, mod_part = pl.pallas_call(
         backward_kernel,
         grid=(fd,),
         out_shape=(
             jax.ShapeDtypeStruct(hidden.shape, BF16),
-            jax.ShapeDtypeStruct(head_weight.shape, F32),
+            jax.ShapeDtypeStruct(head_shape, F32),
             jax.ShapeDtypeStruct((fd, 2, width), F32),
         ),
         in_specs=[
@@ -526,29 +588,30 @@
             mod_frame,
             vmem,
             stat_frame,
+            stat_frame,
             pl.BlockSpec((1, C, tok * PATCH), lambda f: (f, 0, 0)),
         ],
-        out_specs=(by_frame, pl.BlockSpec(head_weight.shape, lambda f: (0, 0)), mod_frame),
+        out_specs=(by_frame, pl.BlockSpec(head_shape, lambda f: (0,) * 5), mod_frame),
         scratch_shapes=[
             pltpu.VMEM((tok, width), BF16),
             pltpu.VMEM((tok, width), F32),
             pltpu.VMEM((size, size), BF16),
             pltpu.VMEM((C * PATCH, C * PATCH), BF16),
+            pltpu.VMEM((C * PATCH, width), F32),
             pltpu.VMEM((8, width), F32),
-            pltpu.VMEM((8, width), F32),
+            pltpu.VMEM((tok, LANES), F32),
+            pltpu.VMEM((tok, LANES), F32),
+            pltpu.VMEM((tok, LANES), F32),
         ],
         compiler_params=params(),
         name="backward",
-    )(hidden, modulation, head_weight, stats, upstream)
-
-    head_rows = head_part.size // (n_tm * n_eval * LANES)
-    mod_rows = mod_part.size // (n_eval * LANES)
-    head_shape = (n_eval, n_tm, head_rows, LANES)
-    mod_shape = (n_eval, mod_rows, LANES)
+    )(hidden, modulation, head_weight, center, inv_std, upstream)
+
+    mod_shape = (n_eval, per, 2, width)
     e_sem, t_sem = dma((n_eval - 1,)), dma((n_tm - 1,))
     head_grad, mod_grad = pl.pallas_call(
         functools.partial(sum_kernel, n_tm, n_eval),
-        out_shape=(jax.ShapeDtypeStruct(head_shape, F32), jax.ShapeDtypeStruct(mod_shape, F32)),
+        out_shape=(jax.ShapeDtypeStruct(head_weight.shape, F32), jax.ShapeDtypeStruct(mod_shape, F32)),
         in_specs=[vmem, vmem],
         out_specs=(vmem, vmem),
         scratch_shapes=[
@@ -562,8 +625,8 @@
         ],
         compiler_params=params(2),
         name="sums",
-    )(head_part.reshape(head_shape), mod_part.reshape(mod_shape))
-    return (d_hidden, head_grad.reshape(head_part.shape), mod_grad.reshape(mod_part.shape))
+    )(head_part, mod_part.reshape(mod_shape))
+    return (d_hidden, head_grad, mod_grad.reshape(mod_part.shape))
 
 
 def solution(mesh):

time: 199 us -> 174 us (0.87)
  Pallas kernels: 190 us -> 169 us
  local copies, waits for them, and re-layouts: 8.38 us -> 4.7 us
    pallas_call x1, Pallas kernels: 67.9 us -> 56 us  [per_device(): pl.pallas_call(functools.partial(forward_kernel, n_tm, n_eval, n_blk), gr...]
    pallas_call x1, Pallas kernels: 47.5 us -> 38.6 us  [per_device(): pl.pallas_call(backward_kernel, grid=(fd,), out_shape=(jax.ShapeDtypeStru...]
    reshape x4 -> x0, local copies, waits for them, and re-layouts: 7.07 us -> none  [the longest x1 1.8 us: per_device(): head_grad.reshape(head_part.shape)]
    unnamed x0 -> x2, local copies, waits for them, and re-layouts: none -> 3.39 us
where the time goes in v2:
time: 174 us
  Pallas kernels  169 us (97%)
  local copies, waits for them, and re-layouts  4.7 us (3%)
    pallas_call x1, Pallas kernels, per_device(): pl.pallas_call(functools.partial(forward_kernel, n_tm, n_eval, n_blk), gr...  56 us
    pallas_call x1, Pallas kernels, per_device(): pl.pallas_call(backward_kernel, grid=(fd,), out_shape=(jax.ShapeDtypeStru...  38.6 us
    pallas_call x1, Pallas kernels, per_device(): pl.pallas_call(functools.partial(reduce_kernel, n_tm, n_eval, n_blk), out...  37 us
    pallas_call x1, Pallas kernels, per_device(): pl.pallas_call(functools.partial(sum_kernel, n_tm, n_eval), out_shape=(ja...  29.6 us
    pallas_call x1, Pallas kernels, per_device(): pl.pallas_call(functools.partial(window_kernel, float(WIN * C * pixel_blo...  7.39 us

profile of v2, /device:TPU:1, one launch (start us, length us, event | category | flops | bytes accessed | tf_op | source)
XLA Modules:
  0.0 173.9 jit_solution(17385539281196431066)
XLA Ops:
  0.6 1.3 broadcast_in_dim.2.times
  1.9 56.0 %forward.1 = (f32[8,128]{1,0:T(8,128)}, f32[16,256,128]{2,1,0:T(8,128)}, f32[16,256,128]{2,1,0:T(8,128)}) custom-call(s32[8]{0:T(128)} %starts.3, bf16[16,256,1536]{2,1,0:T(8,128)(2,1)} %hidden.3, f32[16,2,1536]{2,1,0:T(2,128)} %modulation.3, bf16[64,1536]{1,0:T(8,128)(2,1)} %weight.3, bf16[8,21,16,512]{3,2,1,0:T(8,128)(2,1)} %real.3), custom_call_target="tpu_custom_call" | custom-call | tf_op jit(solution)/shard_map/forward/pallas_call | solution.py:513
  58.0 7.4 %windows.1 = f32[128,16,512]{2,1,0:T(8,128)} custom-call(s32[8]{0:T(128)} %starts.3, f32[8,128]{1,0:T(8,128)} %get-tuple-element.13.totals, s32[8,128]{1,0:T(8,128)} %broadcast_in_dim.2.times, bf16[8,21,16,512]{3,2,1,0:T(8,128)(2,1)} %real.3, bf16[8,21,16,512]{3,2,1,0:T(8,128)(2,1)} %fake.1), custom_call_target="tpu_custom_call" | custom-call | tf_op jit(solution)/shard_map/windows/pallas_call | solution.py:545
  65.4 37.0 %reduce.1.upstream = bf16[16,16,1024]{2,1,0:T(8,128)(2,1)} custom-call(f32[8,16,16,512]{3,2,1,0:T(8,128)} %bitcast.3), custom_call_target="tpu_custom_call" | custom-call | tf_op jit(solution)/shard_map/reduce/pallas_call | solution.py:554
  102.4 38.6 %backward.1 = (bf16[16,256,1536]{2,1,0:T(8,128)(2,1)}, f32[4,8,3,8,128]{4,3,2,1,0:T(8,128)}, f32[16,2,1536]{2,1,0:T(2,128)}) custom-call(bf16[16,256,1536]{2,1,0:T(8,128)(2,1)} %hidden.3, f32[16,2,1536]{2,1,0:T(2,128)} %modulation.3, bf16[64,1536]{1,0:T(8,128)(2,1)} %weight.3, f32[16,256,128]{2,1,0:T(8,128)} %get-tuple-element.11.center, ...), custom_call_target="tpu_custom_call" | custom-call | tf_op jit(solution)/shard_map/backward/pallas_call | solution.py:578
  141.0 29.6 %sums.1 = (f32[64,1536]{1,0:T(8,128)}, f32[4,4,2,1536]{3,2,1,0:T(2,128)}) custom-call(f32[4,8,3,8,128]{4,3,2,1,0:T(8,128)} %get-tuple-element.15.head, f32[4,4,2,1536]{3,2,1,0:T(2,128)} %bitcast.5), custom_call_target="tpu_custom_call" | custom-call | tf_op jit(solution)/shard_map/sums/pallas_call | solution.py:612
  170.6 1.8 %copy.12 = f32[64,1536]{1,0:T(8,128)} copy(f32[64,1536]{1,0:T(8,128)} %get-tuple-element.23) | data formatting | bytes 786432
  172.3 1.6 copy.13

commit v3 on v2

--- a/solution.py
+++ b/solution.py
@@ -13,7 +13,9 @@
 TOK = 1024
 EPS = 1e-06
 LANES = 128
-ROWS = 16
+ROWS = 32
+SUB = 8
+PAIR = 2
 MESH = pl.DeviceIdType.MESH
 VMEM_LIMIT = 56 * 1024 * 1024
 F32 = jnp.float32
@@ -52,13 +54,17 @@
     return pl.ds(pl.multiple_of(i * ROWS, ROWS), ROWS)
 
 
+def by_sublane(block):
+    return block.reshape(block.shape[0] // SUB, SUB, block.shape[1])
+
+
 def dot(a, b, dims=((1,), (0,))):
     return lax.dot_general(a, b, (dims, ((), ())), preferred_element_type=F32)
 
 
 def forward_kernel(
     n_tm, n_eval, n_blk, starts, hidden, modulation, weight, real, totals, center, inv_std,
-    adapted, part, perm, rows, mine, latent, sums, out_send, out_recv, x_send, x_recv, c_send, c_recv, s_send, s_recv,
+    adapted, part, shift8, scale8, perm, rows, mine, latent, sums, out_send, out_recv, x_send, x_recv, c_send, c_recv, s_send, s_recv,
 ):
     frame = pl.program_id(0)
     frames = pl.num_programs(0)
@@ -86,62 +92,78 @@
         perm[...] = pixel_permutation(False)
         rows[...] = row_permutation(False)
 
-    shift = modulation[0, 0:1, :]
-    scale = 1.0 + modulation[0, 1:2, :]
     tiles = [slice(i * LANES, (i + 1) * LANES) for i in range(width // LANES)]
+    shift8[...] = jnp.broadcast_to(modulation[0, 0:1, :], shift8.shape)
+    scale8[...] = jnp.broadcast_to(1.0 + modulation[0, 1:2, :], scale8.shape)
 
     def row_sums(body):
         def step(i, carry):
             at = chunk_rows(i)
-            acc = body(at, tiles[0])
+            add_tile = body(at)
+            acc = add_tile(tiles[0])
             for tile in tiles[1:]:
-                acc = acc + body(at, tile)
+                acc = acc + add_tile(tile)
             part[at, :] = acc
             return carry
 
-        lax.fori_loop(0, tok // ROWS, step, 0, unroll=4)
+        lax.fori_loop(0, tok // ROWS, step, 0, unroll=2)
         return jnp.broadcast_to(jnp.sum(part[...], axis=1, keepdims=True) * (1.0 / width), (tok, LANES))
 
-    def squares(at, tile):
-        shifted = hidden[0, at, tile].astype(F32) - center[0, at, :]
-        return shifted * shifted
-
-    center[0] = row_sums(lambda at, tile: hidden[0, at, tile].astype(F32))
+    def squares(at):
+        middle = center[0, at, :]
+
+        def body(tile):
+            shifted = hidden[0, at, tile].astype(F32) - middle
+            return shifted * shifted
+
+        return body
+
+    center[0] = row_sums(lambda at: lambda tile: hidden[0, at, tile].astype(F32))
     inv_std[0] = lax.rsqrt(row_sums(squares) + EPS)
+    turn = frame % PAIR
 
     def adapt(i, carry):
         at = chunk_rows(i)
+        middle, inv = center[0, at, :], inv_std[0, at, :]
         for tile in tiles:
-            normed = (hidden[0, at, tile].astype(F32) - center[0, at, :]) * inv_std[0, at, :]
-            adapted[at, tile] = (normed * scale[:, tile] + shift[:, tile]).astype(BF16)
+            normed = by_sublane((hidden[0, at, tile].astype(F32) - middle) * inv)
+            shaped = normed * scale8[:, tile] + shift8[:, tile]
+            adapted[turn, at, tile] = shaped.reshape(ROWS, LANES).astype(BF16)
         return carry
 
-    lax.fori_loop(0, tok // ROWS, adapt, 0, unroll=4)
-    out = dot(weight[...], adapted[...], ((1,), (1,))).astype(BF16)
-    grouped = dot(rows[...], out).astype(BF16)
-    pixels = []
-    for j in range(tok // LANES):
-        tile = grouped[:, j * LANES : (j + 1) * LANES]
-        wide = jnp.concatenate([tile[s * C : (s + 1) * C] for s in range(PATCH)], axis=1)
-        pixels.append(dot(wide, perm[...]).astype(BF16))
-    pixels = jnp.concatenate(pixels, axis=1)
-    pixel_block = mine.shape[3]
-    target = frame % n_eval
-    place = frame // n_eval
-    for b in range(n_blk):
-        mine[frame, b] = pixels[:, b * pixel_block : (b + 1) * pixel_block]
-    for b in range(n_blk):
-        owner = e * n_blk + b
-        own = (owner == t) & (target == e)
-        dst = latent.at[target, place, t]
-
-        @pl.when(own)
-        def _():
-            pltpu.make_async_copy(mine.at[frame, b], dst, out_recv.at[place, t]).start()
-
-        @pl.when(jnp.logical_not(own))
-        def _():
-            remote(mine.at[frame, b], dst, out_send.at[frame, b], out_recv.at[place, t], (owner, target)).start()
+    lax.fori_loop(0, tok // ROWS, adapt, 0, unroll=2)
+
+    @pl.when(turn == PAIR - 1)
+    def _():
+        out = dot(weight[...], adapted[...].reshape(PAIR * tok, width), ((1,), (1,))).astype(BF16)
+        grouped = dot(rows[...], out).astype(BF16)
+        wide = []
+        for j in range(PAIR * tok // LANES):
+            tile = grouped[:, j * LANES : (j + 1) * LANES]
+            wide.append(jnp.concatenate([tile[s * C : (s + 1) * C] for s in range(PATCH)], axis=1))
+        pixels = dot(jnp.concatenate(wide, axis=0), perm[...]).astype(BF16)
+        pixel_block = mine.shape[3]
+        per_tile = PATCH * LANES // pixel_block
+        for p in range(PAIR):
+            f = frame - (PAIR - 1) + p
+            target = f % n_eval
+            place = f // n_eval
+            for b in range(n_blk):
+                row = (p * (tok // LANES) + b // per_tile) * C
+                col = b % per_tile * pixel_block
+                mine[f, b] = pixels[row : row + C, col : col + pixel_block]
+            for b in range(n_blk):
+                owner = e * n_blk + b
+                own = (owner == t) & (target == e)
+                dst = latent.at[target, place, t]
+
+                @pl.when(own)
+                def _():
+                    pltpu.make_async_copy(mine.at[f, b], dst, out_recv.at[place, t]).start()
+
+                @pl.when(jnp.logical_not(own))
+                def _():
+                    remote(mine.at[f, b], dst, out_send.at[f, b], out_recv.at[place, t], (owner, target)).start()
 
     def x_copy(r, d):
         there = 2 * ((x + d) % n_x) + core
@@ -212,23 +234,9 @@
         totals[...] = result
 
 
-def window_kernel(n_pixels, starts, totals, times, real, fake, out):
-    out[...] = jnp.zeros_like(out)
-    level = times[...].astype(F32) / 1000.0 / (totals[...] / n_pixels + 1e-05)
-    for w in range(real.shape[0]):
-        start = starts[w]
-        gain = level[w : w + 1, 0:1]
-
-        def add(k, carry):
-            out[start + k] += gain * (fake[w, k].astype(F32) - real[w, k].astype(F32))
-            return carry
-
-        lax.fori_loop(0, WIN, add, 0, unroll=3)
-
-
 def reduce_kernel(
-    n_tm, n_eval, n_blk, grad, out,
-    from_core, half, from_x, rounded, landed, c_send, c_recv, x_send, x_recv, o_send, o_recv,
+    n_tm, n_eval, n_blk, starts, times, totals, real, fake, out,
+    grad, gain, from_core, half, from_x, rounded, landed, c_send, c_recv, x_send, x_recv, o_send, o_recv,
 ):
     t = lax.axis_index("tm")
     e = lax.axis_index("eval")
@@ -269,19 +277,40 @@
     def order(i):
         return (t + i) % n_tm
 
-    def start_core(i, carry):
-        core_copy(order(i)).start()
-        return carry
-
-    def combine(i, carry):
+    pixel_block = grad.shape[3]
+    n_win = real.shape[0]
+    spread = totals[...] / float(WIN * C * pixel_block * n_tm) + 1e-05
+    for w in range(n_win):
+        level = times[w].astype(F32) / 1000.0
+        gain[w] = jnp.broadcast_to(level / spread[w : w + 1, :], (SUB, LANES))
+
+    def start_core(i):
+        o = order(i)
+
+        def build(j, carry):
+            total = jnp.zeros((C, pixel_block), F32)
+            for w in range(n_win):
+                k = o * fd + j - starts[w]
+                inside = jnp.where((k >= 0) & (k < WIN), 1.0, 0.0)
+                k = jnp.clip(k, 0, WIN - 1)
+                factor = gain[w] * inside
+                factor = jnp.concatenate([factor] * (pixel_block // LANES), axis=1)
+                factor = jnp.concatenate([factor] * (C // SUB), axis=0)
+                total = total + factor * (fake[w, k].astype(F32) - real[w, k].astype(F32))
+            grad[o, j] = total
+            return carry
+
+        lax.fori_loop(0, fd, build, 0)
+        core_copy(o).start()
+
+    def combine(i):
         o = order(i)
         core_copy(o).wait_recv()
         half[o] = grad[o, pl.ds(core * mid, mid)] + from_core[o]
         for d in range(1, n_x):
             x_copy(o, d).start()
-        return carry
-
-    def finish(i, carry):
+
+    def finish(i):
         o = order(i)
         total = half[o, pl.ds(x * per, per)]
         for d in range(1, n_x):
@@ -298,8 +327,6 @@
         def _():
             out_copy(o).start()
 
-        return carry
-
     def drain(i, carry):
         o = order(i)
         core_copy(o).wait_send()
@@ -308,21 +335,26 @@
         when_not((o == t) & (home == e), lambda: out_copy(o).wait_send())
         return carry
 
-    lax.fori_loop(0, n_tm, start_core, 0)
-    lax.fori_loop(0, n_tm, combine, 0)
-    lax.fori_loop(0, n_tm, finish, 0)
+    lag = min(4, n_tm)
+
+    def step(i, carry):
+        pl.when(i < n_tm)(lambda: start_core(i))
+        pl.when((i >= 1) & (i < n_tm + 1))(lambda: combine(i - 1))
+        pl.when(i >= lag)(lambda: finish(i - lag))
+        return carry
+
+    lax.fori_loop(0, n_tm + lag, step, 0)
     lax.fori_loop(0, n_tm, drain, 0)
     for b in range(n_blk):
         for q in range(n_eval):
             pltpu.make_async_copy(rounded.at[0], landed.at[b, q], o_recv.at[b, q]).wait()
-    pixel_block = grad.shape[3]
     for b in range(n_blk):
         out[:, :, b * pixel_block : (b + 1) * pixel_block] = landed[b].reshape(fd, C, pixel_block)
 
 
 def backward_kernel(
     hidden, modulation, weight, center, inv_std, upstream, d_hidden, head_tiles, mod_part,
-    adapted, d_adapted, perm, rows, head, sum_b, part, mean_a, mean_b,
+    adapted, d_adapted, ups, shift8, scale8, perm, rows, head, sum_b, part, mean_a, mean_b,
 ):
     frame = pl.program_id(0)
     tok, width = hidden.shape[1], hidden.shape[2]
@@ -332,15 +364,22 @@
         perm[...] = pixel_permutation(True)
         rows[...] = row_permutation(True)
         head[...] = jnp.zeros_like(head)
-
-    shift = modulation[0, 0:1, :]
+        size = LANES * PATCH
+        fd = ups.shape[0]
+        flat = upstream[...].reshape(fd * C, tok * PATCH)
+        for j in range(tok // LANES):
+            wide = dot(flat[:, j * size : (j + 1) * size], perm[...]).astype(BF16)
+            for f in range(fd):
+                block = [wide[f * C : (f + 1) * C, s * LANES : (s + 1) * LANES] for s in range(PATCH)]
+                ups[f, :, j * LANES : (j + 1) * LANES] = jnp.concatenate(block, axis=0)
+        mixed = dot(rows[...], jnp.concatenate([ups[f] for f in range(fd)], axis=1)).astype(BF16)
+        for f in range(fd):
+            ups[f] = mixed[:, f * tok : (f + 1) * tok]
+
     scale = 1.0 + modulation[0, 1:2, :]
-    size = LANES * PATCH
-    blocks = []
-    for j in range(tok // LANES):
-        wide = dot(upstream[0, :, j * size : (j + 1) * size], perm[...]).astype(BF16)
-        blocks.append(jnp.concatenate([wide[:, s * LANES : (s + 1) * LANES] for s in range(PATCH)], axis=0))
-    up = dot(rows[...], jnp.concatenate(blocks, axis=1)).astype(BF16)
+    shift8[...] = jnp.broadcast_to(modulation[0, 0:1, :], shift8.shape)
+    scale8[...] = jnp.broadcast_to(scale, scale8.shape)
+    up = ups[frame]
     d_adapted[...] = dot(up, weight[...], ((0,), (0,)))
     weight_f32 = weight[...].astype(F32)
     up_sum = jnp.sum(up.astype(F32), axis=1, keepdims=True)
@@ -359,32 +398,33 @@
 
     def gather(i, carry):
         at = chunk_rows(i)
-        acc = jnp.zeros((ROWS, LANES), F32)
+        middle, inv = center[0, at, :], inv_std[0, at, :]
+        acc = jnp.zeros((ROWS // SUB, SUB, LANES), F32)
         for tile in tiles:
-            normed = (hidden[0, at, tile].astype(F32) - center[0, at, :]) * inv_std[0, at, :]
-            scaled = normed * scale[:, tile]
-            adapted[at, tile] = (scaled + shift[:, tile]).astype(BF16)
-            da = d_adapted[at, tile]
+            normed = by_sublane((hidden[0, at, tile].astype(F32) - middle) * inv)
+            scaled = normed * scale8[:, tile]
+            adapted[at, tile] = (scaled + shift8[:, tile]).reshape(ROWS, LANES).astype(BF16)
+            da = by_sublane(d_adapted[at, tile])
             acc = acc + da * scaled
-            cross = da * normed
-            sum_b[:, tile] += cross[0:8] + cross[8:16]
-        part[at, :] = acc
+            sum_b[:, tile] += jnp.sum(da * normed, axis=0)
+        part[at, :] = acc.reshape(ROWS, LANES)
         return carry
 
-    lax.fori_loop(0, tok // ROWS, gather, 0, unroll=4)
+    lax.fori_loop(0, tok // ROWS, gather, 0, unroll=2)
     mean_cross = jnp.sum(part[...], axis=1, keepdims=True) * (1.0 / width)
     mean_b[...] = mean_cross * inv_std[0] * inv_std[0]
     head[...] += dot(up, adapted[...])
 
     def finish(i, carry):
         at = chunk_rows(i)
+        middle, inv, first, second = center[0, at, :], inv_std[0, at, :], mean_a[at, :], mean_b[at, :]
         for tile in tiles:
-            shifted = hidden[0, at, tile].astype(F32) - center[0, at, :]
-            dn = d_adapted[at, tile] * scale[:, tile] * inv_std[0, at, :]
-            d_hidden[0, at, tile] = (dn - mean_a[at, :] - shifted * mean_b[at, :]).astype(BF16)
+            shifted = hidden[0, at, tile].astype(F32) - middle
+            dn = (by_sublane(d_adapted[at, tile]) * scale8[:, tile]).reshape(ROWS, LANES) * inv
+            d_hidden[0, at, tile] = (dn - first - shifted * second).astype(BF16)
         return carry
 
-    lax.fori_loop(0, tok // ROWS, finish, 0, unroll=4)
+    lax.fori_loop(0, tok // ROWS, finish, 0, unroll=2)
     mod_part[0, 1:2, :] = jnp.sum(sum_b[...], axis=0, keepdims=True)
 
     @pl.when(frame == pl.num_programs(0) - 1)
@@ -521,8 +561,10 @@
         in_specs=[smem, by_frame, mod_frame, vmem, vmem],
         out_specs=(pl.BlockSpec((n_win, LANES), lambda f: (0, 0)), stat_frame, stat_frame),
         scratch_shapes=[
-            pltpu.VMEM((tok, width), BF16),
+            pltpu.VMEM((PAIR, tok, width), BF16),
             pltpu.VMEM((tok, LANES), F32),
+            pltpu.VMEM((SUB, width), F32),
+            pltpu.VMEM((SUB, width), F32),
             pltpu.VMEM((size, size), BF16),
             pltpu.VMEM((C * PATCH, C * PATCH), BF16),
             pltpu.VMEM((fd, n_blk, C, pixel_block), BF16),
@@ -541,22 +583,14 @@
         name="forward",
     )(window_start, hidden, modulation, head_weight, real_score)
 
-    frames = fd * n_tm
-    grad = pl.pallas_call(
-        functools.partial(window_kernel, float(WIN * C * pixel_block * n_tm)),
-        out_shape=jax.ShapeDtypeStruct((frames, C, pixel_block), F32),
-        in_specs=[smem, vmem, vmem, vmem, vmem],
-        out_specs=vmem,
-        compiler_params=params(),
-        name="windows",
-    )(window_start, totals, jnp.broadcast_to(timestep[:, None], (n_win, LANES)), real_score, fake_score)
-
     upstream = pl.pallas_call(
         functools.partial(reduce_kernel, n_tm, n_eval, n_blk),
         out_shape=jax.ShapeDtypeStruct((fd, C, tok * PATCH), BF16),
-        in_specs=[vmem],
+        in_specs=[smem, smem, vmem, vmem, vmem],
         out_specs=vmem,
         scratch_shapes=[
+            pltpu.VMEM((n_tm, fd, C, pixel_block), F32),
+            pltpu.VMEM((n_win, SUB, LANES), F32),
             pltpu.VMEM((n_tm, fd // 2, C, pixel_block), F32),
             pltpu.VMEM((n_tm, fd // 2, C, pixel_block), F32),
             pltpu.VMEM((n_tm, extra_x, per, C, pixel_block), F32),
@@ -571,7 +605,7 @@
         ],
         compiler_params=params(1),
         name="reduce",
-    )(grad.reshape(n_tm, fd, C, pixel_block))
+    )(window_start, timestep, totals, real_score, fake_score)
 
     head_tiles = width // LANES * (C * PATCH // 8)
     head_shape = (n_eval, n_tm, pl.cdiv(head_tiles, n_eval * n_tm), 8, LANES)
@@ -589,12 +623,15 @@
             vmem,
             stat_frame,
             stat_frame,
-            pl.BlockSpec((1, C, tok * PATCH), lambda f: (f, 0, 0)),
+            vmem,
         ],
         out_specs=(by_frame, pl.BlockSpec(head_shape, lambda f: (0,) * 5), mod_frame),
         scratch_shapes=[
             pltpu.VMEM((tok, width), BF16),
             pltpu.VMEM((tok, width), F32),
+            pltpu.VMEM((fd, C * PATCH, tok), BF16),
+            pltpu.VMEM((SUB, width), F32),
+            pltpu.VMEM((SUB, width), F32),
             pltpu.VMEM((size, size), BF16),
             pltpu.VMEM((C * PATCH, C * PATCH), BF16),
             pltpu.VMEM((C * PATCH, width), F32),

time: 174 us -> 160 us (0.920)
  Pallas kernels: 169 us -> 155 us
    pallas_call x1 -> x0, Pallas kernels: 7.39 us -> none  [per_device(): pl.pallas_call(functools.partial(window_kernel, float(WIN * C * pixel_blo...]
    pallas_call x1, Pallas kernels: 38.6 us -> 33 us  [per_device(): pl.pallas_call(backward_kernel, grid=(fd,), out_shape=(jax.ShapeDtypeStru...]
    pallas_call x1, Pallas kernels: 37 us -> 41.6 us  [per_device(): pl.pallas_call(functools.partial(reduce_kernel, n_tm, n_eval, n_blk), out...]
    pallas_call x1, Pallas kernels: 56 us -> 53 us  [per_device(): pl.pallas_call(functools.partial(forward_kernel, n_tm, n_eval, n_blk), gr...]
    pallas_call x1, Pallas kernels: 29.6 us -> 27.5 us  [per_device(): pl.pallas_call(functools.partial(sum_kernel, n_tm, n_eval), out_shape=(ja...]
where the time goes in v3:
time: 160 us; the launch traced here: 159 us
  Pallas kernels  155 us (97%)
  local copies, waits for them, and re-layouts  3.39 us (2%)
    pallas_call x1, Pallas kernels, per_device(): pl.pallas_call(functools.partial(forward_kernel, n_tm, n_eval, n_blk), gr...  53 us
    pallas_call x1, Pallas kernels, per_device(): pl.pallas_call(functools.partial(reduce_kernel, n_tm, n_eval, n_blk), out...  41.6 us
    pallas_call x1, Pallas kernels, per_device(): pl.pallas_call(backward_kernel, grid=(fd,), out_shape=(jax.ShapeDtypeStru...  33 us
    pallas_call x1, Pallas kernels, per_device(): pl.pallas_call(functools.partial(sum_kernel, n_tm, n_eval), out_shape=(ja...  27.5 us
    unnamed x2, local copies, waits for them, and re-layouts  3.39 us

profile of v3, /device:TPU:1, one launch (start us, length us, event | category | flops | bytes accessed | tf_op | source)
XLA Modules:
  0.0 159.1 jit_solution(874171978602200303)
XLA Ops:
  0.6 53.0 %forward.1 = (f32[8,128]{1,0:T(8,128)}, f32[16,256,128]{2,1,0:T(8,128)}, f32[16,256,128]{2,1,0:T(8,128)}) custom-call(s32[8]{0:T(128)} %starts.3, bf16[16,256,1536]{2,1,0:T(8,128)(2,1)} %hidden.3, f32[16,2,1536]{2,1,0:T(2,128)} %modulation.3, bf16[64,1536]{1,0:T(8,128)(2,1)} %weight.3, bf16[8,21,16,512]{3,2,1,0:T(8,128)(2,1)} %real.3), custom_call_target="tpu_custom_call" | custom-call | tf_op jit(solution)/shard_map/forward/pallas_call | solution.py:553
  53.6 41.6 %reduce.1.upstream = bf16[16,16,1024]{2,1,0:T(8,128)(2,1)} custom-call(s32[8]{0:T(128)} %starts.3, s32[8]{0:T(128)} %times.1, f32[8,128]{1,0:T(8,128)} %get-tuple-element.13.totals, bf16[8,21,16,512]{3,2,1,0:T(8,128)(2,1)} %real.3, bf16[8,21,16,512]{3,2,1,0:T(8,128)(2,1)} %fake.1), custom_call_target="tpu_custom_call" | custom-call | tf_op jit(solution)/shard_map/reduce/pallas_call | solution.py:586
  95.3 33.0 %backward.1 = (bf16[16,256,1536]{2,1,0:T(8,128)(2,1)}, f32[4,8,3,8,128]{4,3,2,1,0:T(8,128)}, f32[16,2,1536]{2,1,0:T(2,128)}) custom-call(bf16[16,256,1536]{2,1,0:T(8,128)(2,1)} %hidden.3, f32[16,2,1536]{2,1,0:T(2,128)} %modulation.3, bf16[64,1536]{1,0:T(8,128)(2,1)} %weight.3, f32[16,256,128]{2,1,0:T(8,128)} %get-tuple-element.11.center, ...), custom_call_target="tpu_custom_call" | custom-call | tf_op jit(solution)/shard_map/backward/pallas_call | solution.py:612
  128.3 27.5 %sums.1 = (f32[64,1536]{1,0:T(8,128)}, f32[4,4,2,1536]{3,2,1,0:T(2,128)}) custom-call(f32[4,8,3,8,128]{4,3,2,1,0:T(8,128)} %get-tuple-element.15.head, f32[4,4,2,1536]{3,2,1,0:T(2,128)} %bitcast.3), custom_call_target="tpu_custom_call" | custom-call | tf_op jit(solution)/shard_map/sums/pallas_call | solution.py:649
  155.8 1.8 %copy.12 = f32[64,1536]{1,0:T(8,128)} copy(f32[64,1536]{1,0:T(8,128)} %get-tuple-element.23) | data formatting | bytes 786432
  157.5 1.6 %copy.13 = f32[16,2,1536]{2,1,0:T(2,128)} copy(f32[16,2,1536]{2,1,0:T(2,128)} %bitcast.2) | data formatting | bytes 393216

commit v4 on v3

--- a/solution.py
+++ b/solution.py
@@ -16,6 +16,7 @@
 ROWS = 32
 SUB = 8
 PAIR = 2
+LAG = 5
 MESH = pl.DeviceIdType.MESH
 VMEM_LIMIT = 56 * 1024 * 1024
 F32 = jnp.float32
@@ -235,157 +236,188 @@
 
 
 def reduce_kernel(
-    n_tm, n_eval, n_blk, starts, times, totals, real, fake, out,
+    n_tm, n_eval, n_blk, starts, times, totals, real, fake, hidden, modulation, weight, center, inv_std,
+    ups, mean_b, head_out, mod_out,
     grad, gain, from_core, half, from_x, rounded, landed, c_send, c_recv, x_send, x_recv, o_send, o_recv,
+    adapted, d_adapted, shift8, scale8, perm, rows, head, sum_b, part, head_tiles, mod_part, *sum_scratch,
 ):
+    step = pl.program_id(0)
     t = lax.axis_index("tm")
     e = lax.axis_index("eval")
     n_x = n_eval // 2
     x, core = e // 2, e % 2
     partner = 2 * x + 1 - core
-    fd = grad.shape[1]
-    per = fd // n_eval
-    mid = fd // 2
+    fd = grad.shape[0]
+    owners = n_tm // n_eval
+    mid = n_tm // 2
     home = t // n_blk
     slot = t % n_blk
-    quarter = core * n_x + x
-
-    for other in range(n_eval):
-        when_not(other == e, lambda: greet((t, other)))
+    pixel_block = grad.shape[3]
+    n_win = real.shape[0]
+    tok, width = hidden.shape[1], hidden.shape[2]
+
+    @pl.when(step == 0)
+    def _():
+        group = t // owners
+        reducer = 2 * (group % n_x) + group // n_x
+        for other in range(n_eval):
+            when_not(other == e, lambda: greet((t, other)))
+        for other in range(n_tm):
+            when_not(other == t, lambda: greet((other, e)))
         for b in range(n_blk):
-            when_not((e * n_blk + b == t) & (other == e), lambda: greet((e * n_blk + b, other)))
-    own_home = jnp.where(home == e, 1, 0)
-    pl.semaphore_wait(pltpu.get_barrier_semaphore(), n_eval - 1 + n_tm - own_home)
-
-    def core_copy(o):
+            when_not((e * n_blk + b == t) & (reducer == e), lambda: greet((e * n_blk + b, reducer)))
+        own = jnp.where((home == e) & (reducer == e), 1, 0)
+        pl.semaphore_wait(pltpu.get_barrier_semaphore(), n_eval - 1 + n_tm - 1 + owners - own)
+        spread = totals[...] / float(WIN * C * pixel_block * n_tm) + 1e-05
+        for w in range(n_win):
+            level = times[w].astype(F32) / 1000.0
+            gain[w] = jnp.broadcast_to(level / spread[w : w + 1, :], (SUB, LANES))
+        head[...] = jnp.zeros_like(head)
+        perm[...] = pixel_permutation(True)
+        rows[...] = row_permutation(True)
+
+    def core_copy(j):
         return remote(
-            grad.at[o, pl.ds((1 - core) * mid, mid)], from_core.at[o], c_send.at[o], c_recv.at[o], (t, partner)
+            grad.at[j, pl.ds((1 - core) * mid, mid)], from_core.at[j], c_send.at[j], c_recv.at[j], (t, partner)
         )
 
-    def x_copy(o, d):
+    def x_copy(j, d):
         there = (x + d) % n_x
         return remote(
-            half.at[o, pl.ds(there * per, per)], from_x.at[o, d - 1], x_send.at[o, d - 1], x_recv.at[o, d - 1],
+            half.at[j, pl.ds(there * owners, owners)], from_x.at[j, d - 1], x_send.at[j, d - 1], x_recv.at[j, d - 1],
             (t, 2 * there + core),
         )
 
-    def out_copy(o):
+    def owner_of(r):
+        return (core * n_x + x) * owners + r
+
+    def out_copy(j, r):
         return remote(
-            rounded.at[o], landed.at[slot, quarter], o_send.at[o], o_recv.at[slot, quarter], (o, home)
+            rounded.at[j, r], landed.at[j, slot], o_send.at[j, r], o_recv.at[j, slot], (owner_of(r), home)
         )
 
-    def order(i):
-        return (t + i) % n_tm
-
-    pixel_block = grad.shape[3]
-    n_win = real.shape[0]
-    spread = totals[...] / float(WIN * C * pixel_block * n_tm) + 1e-05
-    for w in range(n_win):
-        level = times[w].astype(F32) / 1000.0
-        gain[w] = jnp.broadcast_to(level / spread[w : w + 1, :], (SUB, LANES))
-
-    def start_core(i):
-        o = order(i)
-
-        def build(j, carry):
+    @pl.when(step < fd)
+    def _():
+        def build(o, carry):
             total = jnp.zeros((C, pixel_block), F32)
             for w in range(n_win):
-                k = o * fd + j - starts[w]
+                k = o * fd + step - starts[w]
                 inside = jnp.where((k >= 0) & (k < WIN), 1.0, 0.0)
                 k = jnp.clip(k, 0, WIN - 1)
                 factor = gain[w] * inside
                 factor = jnp.concatenate([factor] * (pixel_block // LANES), axis=1)
                 factor = jnp.concatenate([factor] * (C // SUB), axis=0)
                 total = total + factor * (fake[w, k].astype(F32) - real[w, k].astype(F32))
-            grad[o, j] = total
+            grad[step, o] = total
             return carry
 
-        lax.fori_loop(0, fd, build, 0)
-        core_copy(o).start()
-
-    def combine(i):
-        o = order(i)
-        core_copy(o).wait_recv()
-        half[o] = grad[o, pl.ds(core * mid, mid)] + from_core[o]
+        lax.fori_loop(0, n_tm, build, 0)
+        core_copy(step).start()
+
+    @pl.when((step >= 1) & (step < fd + 1))
+    def _():
+        j = step - 1
+        core_copy(j).wait_recv()
+        half[j] = grad[j, pl.ds(core * mid, mid)] + from_core[j]
         for d in range(1, n_x):
-            x_copy(o, d).start()
-
-    def finish(i):
-        o = order(i)
-        total = half[o, pl.ds(x * per, per)]
+            x_copy(j, d).start()
+
+    @pl.when((step >= LAG - 2) & (step < fd + LAG - 2))
+    def _():
+        j = step - (LAG - 2)
+        total = half[j, pl.ds(x * owners, owners)]
         for d in range(1, n_x):
-            x_copy(o, d).wait_recv()
-            total = total + from_x[o, d - 1]
-        rounded[o] = total.astype(BF16)
-        own = (o == t) & (home == e)
-
-        @pl.when(own)
-        def _():
-            pltpu.make_async_copy(rounded.at[o], landed.at[slot, quarter], o_recv.at[slot, quarter]).start()
-
-        @pl.when(jnp.logical_not(own))
-        def _():
-            out_copy(o).start()
-
-    def drain(i, carry):
-        o = order(i)
-        core_copy(o).wait_send()
-        for d in range(1, n_x):
-            x_copy(o, d).wait_send()
-        when_not((o == t) & (home == e), lambda: out_copy(o).wait_send())
-        return carry
-
-    lag = min(4, n_tm)
-
-    def step(i, carry):
-        pl.when(i < n_tm)(lambda: start_core(i))
-        pl.when((i >= 1) & (i < n_tm + 1))(lambda: combine(i - 1))
-        pl.when(i >= lag)(lambda: finish(i - lag))
-        return carry
-
-    lax.fori_loop(0, n_tm + lag, step, 0)
-    lax.fori_loop(0, n_tm, drain, 0)
-    for b in range(n_blk):
-        for q in range(n_eval):
-            pltpu.make_async_copy(rounded.at[0], landed.at[b, q], o_recv.at[b, q]).wait()
-    for b in range(n_blk):
-        out[:, :, b * pixel_block : (b + 1) * pixel_block] = landed[b].reshape(fd, C, pixel_block)
+            x_copy(j, d).wait_recv()
+            total = total + from_x[j, d - 1]
+        rounded[j] = total.astype(BF16)
+        for r in range(owners):
+            own = (owner_of(r) == t) & (home == e)
+
+            @pl.when(own)
+            def _():
+                pltpu.make_async_copy(rounded.at[j, r], landed.at[j, slot], o_recv.at[j, slot]).start()
+
+            @pl.when(jnp.logical_not(own))
+            def _():
+                out_copy(j, r).start()
+
+    @pl.when(step >= LAG)
+    def _():
+        frame = step - LAG
+        for b in range(n_blk):
+            pltpu.make_async_copy(rounded.at[0, 0], landed.at[frame, b], o_recv.at[frame, b]).wait()
+        size = LANES * PATCH
+        flat = jnp.concatenate([landed[frame, b] for b in range(n_blk)], axis=1)
+        wide = jnp.concatenate([flat[:, j * size : (j + 1) * size] for j in range(tok // LANES)], axis=0)
+        wide = dot(wide, perm[...]).astype(BF16)
+        blocks = []
+        for j in range(tok // LANES):
+            block = wide[j * C : (j + 1) * C]
+            blocks.append(jnp.concatenate([block[:, s * LANES : (s + 1) * LANES] for s in range(PATCH)], axis=0))
+        up = dot(rows[...], jnp.concatenate(blocks, axis=1)).astype(BF16)
+        ups[0] = up
+        shift8[...] = jnp.broadcast_to(modulation[0, 0:1, :], shift8.shape)
+        scale8[...] = jnp.broadcast_to(1.0 + modulation[0, 1:2, :], scale8.shape)
+        d_adapted[...] = dot(up, weight[...], ((0,), (0,)))
+        up_sum = jnp.sum(up.astype(F32), axis=1, keepdims=True)
+        per = fd // n_eval
+        mod_part[frame // per, frame % per, 0:1, :] = jnp.sum(weight[...].astype(F32) * up_sum, axis=0, keepdims=True)
+        sum_b[...] = jnp.zeros_like(sum_b)
+        tiles = [slice(i * LANES, (i + 1) * LANES) for i in range(width // LANES)]
+
+        def gather(i, carry):
+            at = chunk_rows(i)
+            middle, inv = center[0, at, :], inv_std[0, at, :]
+            acc = jnp.zeros((ROWS // SUB, SUB, LANES), F32)
+            for tile in tiles:
+                normed = by_sublane((hidden[0, at, tile].astype(F32) - middle) * inv)
+                scaled = normed * scale8[:, tile]
+                adapted[at, tile] = (scaled + shift8[:, tile]).reshape(ROWS, LANES).astype(BF16)
+                da = by_sublane(d_adapted[at, tile])
+                acc = acc + da * scaled
+                sum_b[:, tile] += jnp.sum(da * normed, axis=0)
+            part[at, :] = acc.reshape(ROWS, LANES)
+            return carry
+
+        lax.fori_loop(0, tok // ROWS, gather, 0, unroll=2)
+        mean_cross = jnp.sum(part[...], axis=1, keepdims=True) * (1.0 / width)
+        mean_b[0] = mean_cross * inv_std[0] * inv_std[0]
+        head[...] += dot(up, adapted[...])
+        mod_part[frame // per, frame % per, 1:2, :] = jnp.sum(sum_b[...], axis=0, keepdims=True)
+
+    @pl.when(step == pl.num_programs(0) - 1)
+    def _():
+        per = head_tiles.shape[2]
+        place = 0
+        for col in range(0, width, LANES):
+            for r in range(0, head.shape[0], SUB):
+                head_tiles[place // (per * n_tm), place // per % n_tm, place % per] = head[r : r + SUB, col : col + LANES]
+                place += 1
+        for place in range(place, n_eval * n_tm * per):
+            head_tiles[place // (per * n_tm), place // per % n_tm, place % per] = jnp.zeros((SUB, LANES), F32)
+        sum_parts(n_tm, n_eval, head_tiles, mod_part, head_out, mod_out, *sum_scratch)
+
+        def drain(j, carry):
+            core_copy(j).wait_send()
+            for d in range(1, n_x):
+                x_copy(j, d).wait_send()
+            for r in range(owners):
+                when_not((owner_of(r) == t) & (home == e), lambda: out_copy(j, r).wait_send())
+            return carry
+
+        lax.fori_loop(0, fd, drain, 0)
 
 
 def backward_kernel(
-    hidden, modulation, weight, center, inv_std, upstream, d_hidden, head_tiles, mod_part,
-    adapted, d_adapted, ups, shift8, scale8, perm, rows, head, sum_b, part, mean_a, mean_b,
+    hidden, modulation, weight, center, inv_std, ups, mean_b, d_hidden, d_adapted, scale8, mean_a
 ):
-    frame = pl.program_id(0)
     tok, width = hidden.shape[1], hidden.shape[2]
-
-    @pl.when(frame == 0)
-    def _():
-        perm[...] = pixel_permutation(True)
-        rows[...] = row_permutation(True)
-        head[...] = jnp.zeros_like(head)
-        size = LANES * PATCH
-        fd = ups.shape[0]
-        flat = upstream[...].reshape(fd * C, tok * PATCH)
-        for j in range(tok // LANES):
-            wide = dot(flat[:, j * size : (j + 1) * size], perm[...]).astype(BF16)
-            for f in range(fd):
-                block = [wide[f * C : (f + 1) * C, s * LANES : (s + 1) * LANES] for s in range(PATCH)]
-                ups[f, :, j * LANES : (j + 1) * LANES] = jnp.concatenate(block, axis=0)
-        mixed = dot(rows[...], jnp.concatenate([ups[f] for f in range(fd)], axis=1)).astype(BF16)
-        for f in range(fd):
-            ups[f] = mixed[:, f * tok : (f + 1) * tok]
-
     scale = 1.0 + modulation[0, 1:2, :]
-    shift8[...] = jnp.broadcast_to(modulation[0, 0:1, :], shift8.shape)
     scale8[...] = jnp.broadcast_to(scale, scale8.shape)
-    up = ups[frame]
+    up = ups[0]
     d_adapted[...] = dot(up, weight[...], ((0,), (0,)))
-    weight_f32 = weight[...].astype(F32)
-    up_sum = jnp.sum(up.astype(F32), axis=1, keepdims=True)
-    mod_part[0, 0:1, :] = jnp.sum(weight_f32 * up_sum, axis=0, keepdims=True)
-
-    level = jnp.sum(weight_f32 * scale, axis=1, keepdims=True) * (1.0 / width)
+
+    level = jnp.sum(weight[...].astype(F32) * scale, axis=1, keepdims=True) * (1.0 / width)
     rest = jnp.broadcast_to(level, (level.shape[0], LANES))
     total = jnp.zeros((tok, LANES), F32)
     for _ in range(3):
@@ -393,31 +425,11 @@
         total = total + dot(up, term, ((0,), (0,)))
         rest = rest - term.astype(F32)
     mean_a[...] = total * inv_std[0]
-    sum_b[...] = jnp.zeros_like(sum_b)
     tiles = [slice(i * LANES, (i + 1) * LANES) for i in range(width // LANES)]
-
-    def gather(i, carry):
-        at = chunk_rows(i)
-        middle, inv = center[0, at, :], inv_std[0, at, :]
-        acc = jnp.zeros((ROWS // SUB, SUB, LANES), F32)
-        for tile in tiles:
-            normed = by_sublane((hidden[0, at, tile].astype(F32) - middle) * inv)
-            scaled = normed * scale8[:, tile]
-            adapted[at, tile] = (scaled + shift8[:, tile]).reshape(ROWS, LANES).astype(BF16)
-            da = by_sublane(d_adapted[at, tile])
-            acc = acc + da * scaled
-            sum_b[:, tile] += jnp.sum(da * normed, axis=0)
-        part[at, :] = acc.reshape(ROWS, LANES)
-        return carry
-
-    lax.fori_loop(0, tok // ROWS, gather, 0, unroll=2)
-    mean_cross = jnp.sum(part[...], axis=1, keepdims=True) * (1.0 / width)
-    mean_b[...] = mean_cross * inv_std[0] * inv_std[0]
-    head[...] += dot(up, adapted[...])
 
     def finish(i, carry):
         at = chunk_rows(i)
-        middle, inv, first, second = center[0, at, :], inv_std[0, at, :], mean_a[at, :], mean_b[at, :]
+        middle, inv, first, second = center[0, at, :], inv_std[0, at, :], mean_a[at, :], mean_b[0, at, :]
         for tile in tiles:
             shifted = hidden[0, at, tile].astype(F32) - middle
             dn = (by_sublane(d_adapted[at, tile]) * scale8[:, tile]).reshape(ROWS, LANES) * inv
@@ -425,34 +437,15 @@
         return carry
 
     lax.fori_loop(0, tok // ROWS, finish, 0, unroll=2)
-    mod_part[0, 1:2, :] = jnp.sum(sum_b[...], axis=0, keepdims=True)
-
-    @pl.when(frame == pl.num_programs(0) - 1)
-    def _():
-        per = head_tiles.shape[2]
-        n_tm = head_tiles.shape[1]
-        place = 0
-        for tile in tiles:
-            for r in range(0, head.shape[0], 8):
-                head_tiles[place // (per * n_tm), place // per % n_tm, place % per] = head[r : r + 8, tile]
-                place += 1
-        for place in range(place, head_tiles.shape[0] * n_tm * per):
-            head_tiles[place // (per * n_tm), place // per % n_tm, place % per] = jnp.zeros((8, LANES), F32)
-
-
-def sum_kernel(
+
+
+def sum_parts(
     n_tm, n_eval, head, mod, head_out, mod_out,
     from_eval, from_tm, mod_in, a_send, a_recv, b_send, b_recv, g_send, g_recv, h_send, h_recv, m_send, m_recv,
     k_send, k_recv, head_all, mod_all, mine,
 ):
     t = lax.axis_index("tm")
     e = lax.axis_index("eval")
-    for other in range(n_eval):
-        when_not(other == e, lambda: greet((t, other)))
-    for other in range(n_tm):
-        when_not(other == t, lambda: greet((other, e)))
-    pl.semaphore_wait(pltpu.get_barrier_semaphore(), n_eval - 1 + n_tm - 1)
-
     def eval_peer(d):
         return (e + d) % n_eval
 
@@ -583,75 +576,57 @@
         name="forward",
     )(window_start, hidden, modulation, head_weight, real_score)
 
-    upstream = pl.pallas_call(
+    head_tiles = width // LANES * (C * PATCH // SUB)
+    head_shape = (n_eval, n_tm, pl.cdiv(head_tiles, n_eval * n_tm), SUB, LANES)
+    mod_shape = (n_eval, per, 2, width)
+    owners = n_tm // n_eval
+    e_sem, t_sem = dma((n_eval - 1,)), dma((n_tm - 1,))
+
+    def late(*shape):
+        return pl.BlockSpec((1,) + shape, lambda i: (jnp.maximum(i - LAG, 0),) + (0,) * len(shape))
+
+    def whole(shape):
+        return pl.BlockSpec(shape, lambda i: (0,) * len(shape))
+
+    ups, mean_b, head_grad, mod_grad = pl.pallas_call(
         functools.partial(reduce_kernel, n_tm, n_eval, n_blk),
-        out_shape=jax.ShapeDtypeStruct((fd, C, tok * PATCH), BF16),
-        in_specs=[smem, smem, vmem, vmem, vmem],
-        out_specs=vmem,
-        scratch_shapes=[
-            pltpu.VMEM((n_tm, fd, C, pixel_block), F32),
-            pltpu.VMEM((n_win, SUB, LANES), F32),
-            pltpu.VMEM((n_tm, fd // 2, C, pixel_block), F32),
-            pltpu.VMEM((n_tm, fd // 2, C, pixel_block), F32),
-            pltpu.VMEM((n_tm, extra_x, per, C, pixel_block), F32),
-            pltpu.VMEM((n_tm, per, C, pixel_block), BF16),
-            pltpu.VMEM((n_blk, n_eval, per, C, pixel_block), BF16),
-            dma((n_tm,)),
-            dma((n_tm,)),
-            dma((n_tm, extra_x)),
-            dma((n_tm, extra_x)),
-            dma((n_tm,)),
-            dma((n_blk, n_eval)),
-        ],
-        compiler_params=params(1),
-        name="reduce",
-    )(window_start, timestep, totals, real_score, fake_score)
-
-    head_tiles = width // LANES * (C * PATCH // 8)
-    head_shape = (n_eval, n_tm, pl.cdiv(head_tiles, n_eval * n_tm), 8, LANES)
-    d_hidden, head_part, mod_part = pl.pallas_call(
-        backward_kernel,
-        grid=(fd,),
+        grid=(fd + LAG,),
         out_shape=(
-            jax.ShapeDtypeStruct(hidden.shape, BF16),
-            jax.ShapeDtypeStruct(head_shape, F32),
-            jax.ShapeDtypeStruct((fd, 2, width), F32),
+            jax.ShapeDtypeStruct((fd, C * PATCH, tok), BF16),
+            jax.ShapeDtypeStruct((fd, tok, LANES), F32),
+            jax.ShapeDtypeStruct(head_weight.shape, F32),
+            jax.ShapeDtypeStruct(mod_shape, F32),
         ),
         in_specs=[
-            by_frame,
-            mod_frame,
-            vmem,
-            stat_frame,
-            stat_frame,
-            vmem,
+            smem, smem, vmem, vmem, vmem,
+            late(tok, width), late(2, width), vmem, late(tok, LANES), late(tok, LANES),
         ],
-        out_specs=(by_frame, pl.BlockSpec(head_shape, lambda f: (0,) * 5), mod_frame),
+        out_specs=(late(C * PATCH, tok), late(tok, LANES), whole(head_weight.shape), whole(mod_shape)),
         scratch_shapes=[
+            pltpu.VMEM((fd, n_tm, C, pixel_block), F32),
+            pltpu.VMEM((n_win, SUB, LANES), F32),
+            pltpu.VMEM((fd, n_tm // 2, C, pixel_block), F32),
+            pltpu.VMEM((fd, n_tm // 2, C, pixel_block), F32),
+            pltpu.VMEM((fd, extra_x, owners, C, pixel_block), F32),
+            pltpu.VMEM((fd, owners, C, pixel_block), BF16),
+            pltpu.VMEM((fd, n_blk, C, pixel_block), BF16),
+            dma((fd,)),
+            dma((fd,)),
+            dma((fd, extra_x)),
+            dma((fd, extra_x)),
+            dma((fd, owners)),
+            dma((fd, n_blk)),
             pltpu.VMEM((tok, width), BF16),
             pltpu.VMEM((tok, width), F32),
-            pltpu.VMEM((fd, C * PATCH, tok), BF16),
             pltpu.VMEM((SUB, width), F32),
             pltpu.VMEM((SUB, width), F32),
             pltpu.VMEM((size, size), BF16),
             pltpu.VMEM((C * PATCH, C * PATCH), BF16),
             pltpu.VMEM((C * PATCH, width), F32),
-            pltpu.VMEM((8, width), F32),
+            pltpu.VMEM((SUB, width), F32),
             pltpu.VMEM((tok, LANES), F32),
-            pltpu.VMEM((tok, LANES), F32),
-            pltpu.VMEM((tok, LANES), F32),
-        ],
-        compiler_params=params(),
-        name="backward",
-    )(hidden, modulation, head_weight, center, inv_std, upstream)
-
-    mod_shape = (n_eval, per, 2, width)
-    e_sem, t_sem = dma((n_eval - 1,)), dma((n_tm - 1,))
-    head_grad, mod_grad = pl.pallas_call(
-        functools.partial(sum_kernel, n_tm, n_eval),
-        out_shape=(jax.ShapeDtypeStruct(head_weight.shape, F32), jax.ShapeDtypeStruct(mod_shape, F32)),
-        in_specs=[vmem, vmem],
-        out_specs=(vmem, vmem),
-        scratch_shapes=[
+            pltpu.VMEM(head_shape, F32),
+            pltpu.VMEM(mod_shape, F32),
             pltpu.VMEM((n_eval - 1,) + head_shape[1:], F32),
             pltpu.VMEM((n_tm - 1,) + head_shape[2:], F32),
             pltpu.VMEM((n_eval - 1,) + mod_shape[1:], F32),
@@ -660,10 +635,31 @@
             pltpu.VMEM(mod_shape, F32),
             pltpu.VMEM(head_shape[1:], F32),
         ],
-        compiler_params=params(2),
-        name="sums",
-    )(head_part, mod_part.reshape(mod_shape))
-    return (d_hidden, head_grad, mod_grad.reshape(mod_part.shape))
+        compiler_params=params(1),
+        name="reduce",
+    )(
+        window_start, timestep, totals, real_score, fake_score,
+        hidden, modulation, head_weight, center, inv_std,
+    )
+
+    d_hidden = pl.pallas_call(
+        backward_kernel,
+        grid=(fd,),
+        out_shape=jax.ShapeDtypeStruct(hidden.shape, BF16),
+        in_specs=[
+            by_frame, mod_frame, vmem, stat_frame, stat_frame,
+            pl.BlockSpec((1, C * PATCH, tok), lambda f: (f, 0, 0)), stat_frame,
+        ],
+        out_specs=by_frame,
+        scratch_shapes=[
+            pltpu.VMEM((tok, width), F32),
+            pltpu.VMEM((SUB, width), F32),
+            pltpu.VMEM((tok, LANES), F32),
+        ],
+        compiler_params=params(),
+        name="backward",
+    )(hidden, modulation, head_weight, center, inv_std, ups, mean_b)
+    return (d_hidden, head_grad, mod_grad.reshape(modulation.shape))
 
 
 def solution(mesh):

time: 160 us -> 149 us (0.931)
  Pallas kernels: 155 us -> 146 us
  local copies, waits for them, and re-layouts: 3.39 us -> 1.43 us
    pallas_call x3 -> x2, Pallas kernels: 102 us -> 93 us  [the longest x1 70.7 us: per_device(): pl.pallas_call(functools.partial(reduce_kernel, n_tm, n_eval, n_blk), gri...]
    unnamed x2 -> x6, local copies, waits for them, and re-layouts: 3.39 us -> 1.43 us
where the time goes in v4:
time: 149 us; the launch traced here: 148 us
  Pallas kernels  146 us (98%)
    pallas_call x1, Pallas kernels, per_device(): pl.pallas_call(functools.partial(reduce_kernel, n_tm, n_eval, n_blk), gri...  70.7 us
    pallas_call x1, Pallas kernels, per_device(): pl.pallas_call(functools.partial(forward_kernel, n_tm, n_eval, n_blk), gr...  53 us
    pallas_call x1, Pallas kernels, per_device(): pl.pallas_call(backward_kernel, grid=(fd,), out_shape=jax.ShapeDtypeStruc...  22.3 us

profile of v4, /device:TPU:1, one launch (start us, length us, event | category | flops | bytes accessed | tf_op | source)
XLA Modules:
  0.0 148.1 jit_solution(5275060798670324216)
XLA Ops:
  0.6 53.0 %forward.1 = (f32[8,128]{1,0:T(8,128)}, f32[16,256,128]{2,1,0:T(8,128)}, f32[16,256,128]{2,1,0:T(8,128)}) custom-call(s32[8]{0:T(128)} %starts.3, bf16[16,256,1536]{2,1,0:T(8,128)(2,1)} %hidden.5, f32[16,2,1536]{2,1,0:T(2,128)} %modulation.5, bf16[64,1536]{1,0:T(8,128)(2,1)} %weight.5, bf16[8,21,16,512]{3,2,1,0:T(8,128)(2,1)} %real.3), custom_call_target="tpu_custom_call" | custom-call | tf_op jit(solution)/shard_map/forward/pallas_call | solution.py:546
  53.6 70.7 %reduce.1 = (bf16[16,64,256]{2,1,0:T(8,128)(2,1)}, f32[16,256,128]{2,1,0:T(8,128)}, f32[64,1536]{1,0:T(8,128)}, f32[4,4,2,1536]{3,2,1,0:T(2,128)}) custom-call(s32[8]{0:T(128)} %starts.3, s32[8]{0:T(128)} %times.1, f32[8,128]{1,0:T(8,128)} %get-tuple-element.12.totals, bf16[8,21,16,512]{3,2,1,0:T(8,128)(2,1)} %real.3, bf16[8,21,16,512]{3,2,1,0:T(8,128)(2,1)} %fake.1, ...), custom_call_target="tpu_custom_call" | custom-call | tf_op jit(solution)/shard_map/reduce/pallas_call | solution.py:591
  124.3 0.0 copy-start
  124.4 0.0 copy-start.1
  124.4 22.3 %backward.1 = bf16[16,256,1536]{2,1,0:T(8,128)(2,1)} custom-call(bf16[16,256,1536]{2,1,0:T(8,128)(2,1)} %hidden.5, f32[16,2,1536]{2,1,0:T(2,128)} %modulation.5, bf16[64,1536]{1,0:T(8,128)(2,1)} %weight.5, f32[16,256,128]{2,1,0:T(8,128)} %get-tuple-element.10.center, f32[16,256,128]{2,1,0:T(8,128)} %get-tuple-element.11.inv_std, ...), custom_call_target="tpu_custom_call" | custom-call | tf_op jit(solution)/shard_map/backward/pallas_call | solution.py:645
  146.7 0.0 copy-done
  146.7 0.7 copy.12
  147.4 0.0 copy-done.1
  147.4 0.7 copy.13
Async XLA Ops:
  124.3 22.3 %copy-start = (f32[64,1536]{1,0:T(8,128)S(1)}, f32[64,1536]{1,0:T(8,128)}, u32[]{:S(2)}) copy-start(f32[64,1536]{1,0:T(8,128)} %get-tuple-element.21) | copy-start | bytes 1179652
  124.4 23.0 %copy-start.1 = (f32[4,4,2,1536]{3,2,1,0:T(2,128)S(1)}, f32[4,4,2,1536]{3,2,1,0:T(2,128)}, u32[]{:S(2)}) copy-start(f32[4,4,2,1536]{3,2,1,0:T(2,128)} %get-tuple-element.16) | copy-start | bytes 589828

commit v5 on v4

--- a/solution.py
+++ b/solution.py
@@ -65,7 +65,7 @@
 
 def forward_kernel(
     n_tm, n_eval, n_blk, starts, hidden, modulation, weight, real, totals, center, inv_std,
-    adapted, part, shift8, scale8, perm, rows, mine, latent, sums, out_send, out_recv, x_send, x_recv, c_send, c_recv, s_send, s_recv,
+    adapted, part, ones, shift8, scale8, perm, rows, mine, latent, sums, out_send, out_recv, x_send, x_recv, c_send, c_recv, s_send, s_recv,
 ):
     frame = pl.program_id(0)
     frames = pl.num_programs(0)
@@ -90,6 +90,7 @@
             when_not(other == e, lambda: greet((t, other)))
         own = jnp.where(source == e, 1, 0)
         pl.semaphore_wait(pltpu.get_barrier_semaphore(), n_tm - own + n_tm - 1 + n_eval - 1)
+        ones[...] = jnp.ones_like(ones)
         perm[...] = pixel_permutation(False)
         rows[...] = row_permutation(False)
 
@@ -119,7 +120,7 @@
 
         return body
 
-    center[0] = row_sums(lambda at: lambda tile: hidden[0, at, tile].astype(F32))
+    center[0] = dot(hidden[0], ones[...]) * (1.0 / width)
     inv_std[0] = lax.rsqrt(row_sums(squares) + EPS)
     turn = frame % PAIR
 
@@ -384,6 +385,11 @@
         mean_b[0] = mean_cross * inv_std[0] * inv_std[0]
         head[...] += dot(up, adapted[...])
         mod_part[frame // per, frame % per, 1:2, :] = jnp.sum(sum_b[...], axis=0, keepdims=True)
+        mod_in, m_send, m_recv = sum_scratch[2], sum_scratch[11], sum_scratch[12]
+        for d in range(1, n_eval):
+            peer = (e + d) % n_eval
+            piece = remote(mod_part.at[peer], mod_in.at[d - 1], m_send.at[d - 1], m_recv.at[d - 1], (t, peer))
+            pl.when(frame == (peer + 1) * per - 1)(lambda: piece.start())
 
     @pl.when(step == pl.num_programs(0) - 1)
     def _():
@@ -419,11 +425,11 @@
 
     level = jnp.sum(weight[...].astype(F32) * scale, axis=1, keepdims=True) * (1.0 / width)
     rest = jnp.broadcast_to(level, (level.shape[0], LANES))
-    total = jnp.zeros((tok, LANES), F32)
+    terms = []
     for _ in range(3):
-        term = rest.astype(BF16)
-        total = total + dot(up, term, ((0,), (0,)))
-        rest = rest - term.astype(F32)
+        terms.append(rest.astype(BF16))
+        rest = rest - terms[-1].astype(F32)
+    total = dot(jnp.concatenate([up] * 3, axis=0), jnp.concatenate(terms, axis=0), ((0,), (0,)))
     mean_a[...] = total * inv_std[0]
     tiles = [slice(i * LANES, (i + 1) * LANES) for i in range(width // LANES)]
 
@@ -460,8 +466,6 @@
 
     for d in range(1, n_eval):
         head_in(d).start()
-    for d in range(1, n_eval):
-        mod_scatter(d).start()
     part = head[e]
     for d in range(1, n_eval):
         head_in(d).wait_recv()
@@ -556,6 +560,7 @@
         scratch_shapes=[
             pltpu.VMEM((PAIR, tok, width), BF16),
             pltpu.VMEM((tok, LANES), F32),
+            pltpu.VMEM((width, LANES), BF16),
             pltpu.VMEM((SUB, width), F32),
             pltpu.VMEM((SUB, width), F32),
             pltpu.VMEM((size, size), BF16),

time: 149 us -> 152 us (1.020)
  Pallas kernels: 146 us -> 149 us
    pallas_call x1, Pallas kernels: 70.7 us -> 72.7 us  [per_device(): pl.pallas_call(functools.partial(reduce_kernel, n_tm, n_eval, n_blk), gri...]
where the time goes in v5:
time: 152 us; the launch traced here: 151 us
  Pallas kernels  149 us (98%)
    pallas_call x1, Pallas kernels, per_device(): pl.pallas_call(functools.partial(reduce_kernel, n_tm, n_eval, n_blk), gri...  72.7 us
    pallas_call x1, Pallas kernels, per_device(): pl.pallas_call(functools.partial(forward_kernel, n_tm, n_eval, n_blk), gr...  54.3 us
    pallas_call x1, Pallas kernels, per_device(): pl.pallas_call(backward_kernel, grid=(fd,), out_shape=jax.ShapeDtypeStruc...  22 us

profile of v5, /device:TPU:1, one launch (start us, length us, event | category | flops | bytes accessed | tf_op | source)
XLA Modules:
  0.0 151.2 jit_solution(18229054822424398476)
XLA Ops:
  0.6 54.3 %forward.1 = (f32[8,128]{1,0:T(8,128)}, f32[16,256,128]{2,1,0:T(8,128)}, f32[16,256,128]{2,1,0:T(8,128)}) custom-call(s32[8]{0:T(128)} %starts.3, bf16[16,256,1536]{2,1,0:T(8,128)(2,1)} %hidden.5, f32[16,2,1536]{2,1,0:T(2,128)} %modulation.5, bf16[64,1536]{1,0:T(8,128)(2,1)} %weight.5, bf16[8,21,16,512]{3,2,1,0:T(8,128)(2,1)} %real.3), custom_call_target="tpu_custom_call" | custom-call | tf_op jit(solution)/shard_map/forward/pallas_call | solution.py:550
  55.0 72.7 %reduce.1 = (bf16[16,64,256]{2,1,0:T(8,128)(2,1)}, f32[16,256,128]{2,1,0:T(8,128)}, f32[64,1536]{1,0:T(8,128)}, f32[4,4,2,1536]{3,2,1,0:T(2,128)}) custom-call(s32[8]{0:T(128)} %starts.3, s32[8]{0:T(128)} %times.1, f32[8,128]{1,0:T(8,128)} %get-tuple-element.12.totals, bf16[8,21,16,512]{3,2,1,0:T(8,128)(2,1)} %real.3, bf16[8,21,16,512]{3,2,1,0:T(8,128)(2,1)} %fake.1, ...), custom_call_target="tpu_custom_call" | custom-call | tf_op jit(solution)/shard_map/reduce/pallas_call | solution.py:596
  127.7 0.0 copy-start
  127.7 0.0 copy-start.1
  127.7 22.0 %backward.1 = bf16[16,256,1536]{2,1,0:T(8,128)(2,1)} custom-call(bf16[16,256,1536]{2,1,0:T(8,128)(2,1)} %hidden.5, f32[16,2,1536]{2,1,0:T(2,128)} %modulation.5, bf16[64,1536]{1,0:T(8,128)(2,1)} %weight.5, f32[16,256,128]{2,1,0:T(8,128)} %get-tuple-element.10.center, f32[16,256,128]{2,1,0:T(8,128)} %get-tuple-element.11.inv_std, ...), custom_call_target="tpu_custom_call" | custom-call | tf_op jit(solution)/shard_map/backward/pallas_call | solution.py:650
  149.8 0.0 copy-done
  149.8 0.7 copy.12
  150.5 0.0 copy-done.1
  150.5 0.7 copy.13
Async XLA Ops:
  127.7 22.1 %copy-start = (f32[64,1536]{1,0:T(8,128)S(1)}, f32[64,1536]{1,0:T(8,128)}, u32[]{:S(2)}) copy-start(f32[64,1536]{1,0:T(8,128)} %get-tuple-element.21) | copy-start | bytes 1179652
  127.7 22.8 %copy-start.1 = (f32[4,4,2,1536]{3,2,1,0:T(2,128)S(1)}, f32[4,4,2,1536]{3,2,1,0:T(2,128)}, u32[]{:S(2)}) copy-start(f32[4,4,2,1536]{3,2,1,0:T(2,128)} %get-tuple-element.16) | copy-start | bytes 589828
